TPU v7x, 512 devices: a whole 4x8x8 slice. The times are simulated.
512 devices in a mesh: vol: 16 (over z_lo, y), img: 32 (over z_hi, x, core).
Axes of the slice: x: 4, y: 8, z: 8 (z_hi: 4, z_lo: 2; z = z_hi * 2 + z_lo), core: 2. Of those that a mesh axis runs over, the one named last changes fastest.
Arguments:
- volume: bfloat16 [256, 256, 256], P('vol', 'img'), may hold values from -6 to 6
- images: bfloat16 [16384, 256, 256], P('img', 'vol'), may hold values from -6 to 6
- bin_lists: int32 [32, 16], P('img'), may hold values from 0 to 63, all different within a row
- bin_planes: int32 [64], replicated, may hold values from 0 to 255
- bin_tilts: float32 [64], replicated, may hold values from -1 to 1
- defocus: float32 [32], replicated, may hold values from 20 to 80
- groups: int32 [16384], P('img'), may hold values from 0 to 31
- precision: float32 [16384], P('img'), may hold values from 1 to 40
Outputs:
- posteriors: float32 [16384, 16], P('img')
- numerator: float32 [256, 256, 256], P('vol', None, 'img')
Inputs may be any that keep to these rules, and one draw needn't show every extreme that they name: `bin_lists`: each row names 16 different bins; every bin is named by some row.
All inputs are finite; a program needn't handle non-finite values.
Results may differ from a plain program's by a relative error of at most 0.02.
Values may be sent and summed in bfloat16 or wider, within the bound.
No kernel may reach another device: no remote copies, remote signals or barrier semaphores. Data moves between devices by JAX's collectives and lax.ppermute only.
A program may use at most 64 MiB of HBM per device.

v0:
```python
import math

import jax
import jax.numpy as jnp
from jax import lax
from jax.sharding import PartitionSpec as P

amplitude = 0.1
phase_part = math.sqrt(0.99)
epsilon = 1e-05


def section_weights(planes, tilt_vals, row_ids, plane_ids, height, reach_planes):
    centered = (row_ids.astype(jnp.float32) - (height - 1) * 0.5) * (2.0 / height)
    depth_pos = planes[:, None] + tilt_vals[:, None] * (reach_planes * centered)[None, :]
    distance = plane_ids.astype(jnp.float32)[None, None, :] - depth_pos[:, :, None]
    return jnp.maximum(0.0, 1.0 - jnp.abs(distance)).astype(jnp.bfloat16)


def ctf_table(defocus, row_ids, height, col_count):
    row_freq = (row_ids.astype(jnp.float32) - height // 2) * (2.0 / height)
    col_freq = (jnp.arange(col_count).astype(jnp.float32) - col_count // 2) * (2.0 / col_count)
    radius_sq = row_freq[:, None] ** 2 + col_freq[None, :] ** 2
    phase_shift = 0.5 * math.pi * defocus[:, None, None] * radius_sq[None, :, :]
    return -(phase_part * jnp.sin(phase_shift) + amplitude * jnp.cos(phase_shift))


def per_device(volume, images, bin_lists, bin_planes, bin_tilts, defocus, groups, precision):
    vol_count = lax.axis_size("vol")
    slab_planes = volume.shape[0]
    image_count, band_rows, col_count = images.shape
    height = band_rows * vol_count
    all_planes = slab_planes * vol_count
    vol_index = lax.axis_index("vol")
    first_plane = vol_index * slab_planes
    first_row = vol_index * band_rows
    bin_count = bin_planes.shape[0]
    picker = (bin_lists[0][:, None] == jnp.arange(bin_count)[None, :]).astype(jnp.float32)
    planes = jnp.dot(picker, bin_planes.astype(jnp.float32), precision=lax.Precision.HIGHEST)
    tilt_vals = jnp.dot(picker, bin_tilts, precision=lax.Precision.HIGHEST)
    reach_planes = float(slab_planes)
    band_ids = first_row + jnp.arange(band_rows)
    band_weights = section_weights(
        planes, tilt_vals, band_ids, jnp.arange(all_planes), height, reach_planes
    )
    slab_weights = section_weights(
        planes,
        tilt_vals,
        jnp.arange(height),
        first_plane + jnp.arange(slab_planes),
        height,
        reach_planes,
    )
    full_slab = lax.all_gather(volume, "img", axis=1, tiled=True)
    templates = lax.psum_scatter(
        jnp.einsum(
            "oyz,zyx->yox", slab_weights, full_slab, preferred_element_type=jnp.float32
        ).astype(jnp.bfloat16),
        "vol",
        scatter_dimension=0,
        tiled=True,
    )
    ctf_rows = ctf_table(defocus, band_ids, height, col_count)
    group_total = ctf_rows.shape[0]
    member = (groups[:, None] == jnp.arange(group_total)[None, :]).astype(jnp.float32)
    ctf_images = jnp.dot(
        member,
        ctf_rows.reshape(group_total, band_rows * col_count),
        precision=lax.Precision.HIGHEST,
    )
    flat_images = images.reshape(image_count, band_rows * col_count)
    weighted = (
        (flat_images.astype(jnp.float32) * ctf_images)
        .astype(jnp.bfloat16)
        .reshape(image_count, band_rows, col_count)
    )
    scores = jnp.einsum("nyx,yox->no", weighted, templates, preferred_element_type=jnp.float32)
    squared = templates.astype(jnp.float32) ** 2
    energy = jnp.einsum(
        "gyx,yox->go", ctf_rows * ctf_rows, squared, precision=lax.Precision.HIGHEST
    )
    scores, energy = lax.psum((scores, energy), "vol")
    energy_rows = jnp.dot(member, energy, precision=lax.Precision.HIGHEST)
    logits = precision[:, None] * scores / jnp.sqrt(energy_rows + epsilon)
    posteriors = jax.nn.softmax(logits, axis=1)
    summed_rows = jnp.einsum(
        "no,nyx->oyx", posteriors.astype(jnp.bfloat16), weighted, preferred_element_type=jnp.float32
    ).astype(jnp.bfloat16)
    backprojected = jnp.einsum(
        "oyz,oyx->zyx", band_weights, summed_rows, preferred_element_type=jnp.float32
    ).astype(jnp.bfloat16)
    arrived = lax.all_to_all(backprojected, "vol", split_axis=0, concat_axis=1, tiled=True)
    numerator = lax.psum_scatter(
        arrived.astype(jnp.float32).astype(jnp.bfloat16), "img", scatter_dimension=2, tiled=True
    ).astype(jnp.float32)
    return (posteriors, numerator)


def solution(mesh):
    placed = (
        P("vol", "img", None),
        P("img", "vol", None),
        P("img", None),
        P(),
        P(),
        P(),
        P("img"),
        P("img"),
    )
    return jax.shard_map(
        per_device,
        mesh=mesh,
        in_specs=placed,
        out_specs=(P("img", None), P("vol", None, "img")),
        check_vma=False,
    )
```

profile of v0, /device:TPU:1, one launch (start us, length us, event | category | flops | bytes accessed | tf_op | source)
XLA Modules:
  0.0 372.1 jit_solution(18418386533021537942)
XLA Ops:
  7.2 0.0 copy-start
  7.2 0.0 all-gather.2.cloned.1.call-start
  7.2 1.5 copy.25
  8.7 0.0 all-gather.2.cloned.1.call-update
  8.7 0.0 reduce-scatter.3.cloned.1.call-start
  8.8 0.0 copy-done
  8.8 0.8 convolution_bitcast_fusion.1
  9.7 0.9 convolution_bitcast_fusion.2
  10.5 0.1 multiply_add_fusion
  10.6 0.1 maximum_convert_fusion.1
  10.7 0.9 copy.26
  11.7 66.2 %all-gather.2.cloned.1.call-done = bf16[16,256,256]{2,0,1:T(8,128)(2,1)} async-done(((bf16[16,8,256]{2,0,1:T(8,128)(2,1)}), bf16[16,256,256]{2,0,1:T(8,128)(2,1)}) %all-gather.2.cloned.1.call-update) | async-done | bytes 2097168 | tf_op jit(solution)/shard_map/all_gather | solution.py:54
  77.9 3.6 convolution_convert_fusion
  81.5 0.0 reduce-scatter.3.cloned.1.call-update
  81.5 0.0 reduce-scatter.5.cloned.1.call-start
  81.6 0.1 broadcast_bitcast_fusion
  81.7 0.0 copy-start.5
  81.7 0.0 copy-start.2
  81.7 6.3 %copy.34 = f32[64,8,16,256]{3,1,2,0:T(8,128)S(1)} copy(bf16[64,8,16,256]{3,2,1,0:T(8,128)(2,1)} %bitcast.53) | data formatting | bytes 12582912
  88.1 0.1 add.114
  88.2 0.0 copy-done.5
  88.2 0.1 multiply_add_fusion.1
  88.3 0.0 copy-done.2
  88.3 7.4 %multiply_convert_fusion = bf16[512,4096]{1,0:T(8,128)(2,1)} fusion(f32[512,4096]{1,0:T(8,128)S(1)} %bitcast.48, f32[4096]{0:T(1024)S(1)} %add.118, f32[32]{0:T(128)S(1)} %broadcast_multiply_fusion, s32[512]{0:T(512)S(1)} %copy-done.2), kind=kOutput, calls=%fused_computation | convolution fusion | flops 810172416 | bytes 12601472 | tf_op jit(solution)/shard_map/dot_general | solution.py:66
  95.6 49.2 %reduce-scatter.3.cloned.1.call-done = bf16[16,16,256]{2,1,0:T(8,128)(2,1)} async-done(((bf16[256,16,256]{2,1,0:T(8,128)(2,1)}), bf16[16,16,256]{2,1,0:T(8,128)(2,1)}) %reduce-scatter.3.cloned.1.call-update) | async-done | bytes 131088 | tf_op jit(solution)/shard_map/reduce_scatter | solution.py:55
  144.9 0.0 copy-start.3
  144.9 0.0 copy-start.4
  144.9 3.4 fusion.13
  148.3 0.0 copy-done.3
  148.3 2.5 convolution_bitcast_fusion
  150.8 47.8 %all-reduce = (f32[32,16]{0,1:T(8,128)S(1)}, f32[512,16]{0,1:T(8,128)S(1)}) all-reduce(f32[32,16]{0,1:T(8,128)S(1)} %convolution_bitcast_fusion, f32[512,16]{0,1:T(8,128)S(1)} %fusion.13), channel_id=1, replica_groups=mesh['vol'=16,'img'=32] {'vol'}, use_global_device_ids=true, to_apply=%region_2.0 | all-reduce | flops 8704 | bytes 69632 | tf_op jit(solution)/shard_map/psum | solution.py:82
  198.6 0.0 copy-done.4
  198.6 0.3 fusion.59
  199.1 0.0 copy-start.1
  199.1 4.8 %convert_bitcast_fusion = bf16[256,16,256]{0,2,1:T(8,128)(2,1)} fusion(bf16[64,16,8,256]{3,2,1,0:T(8,128)(2,1)} %bitcast.50, f32[16,16]{0,1:T(8,128)S(1)} %multiply_add_fusion.1, f32[256]{0:T(256)S(1)} %iota_convert_fusion, f32[512,16]{0,1:T(8,128)S(1)} %fusion.44), kind=kOutput, calls=%fused_computation.7 | convolution fusion | flops 102113280 | bytes 6326272 | tf_op jit(solution)/shard_map/oyz,oyx->zyx/dot_general | solution.py:89
  203.8 3.3 copy.29
  207.2 0.0 copy-done.1
  207.2 29.8 %all_to_all.18 = bf16[256,16,256]{2,1,0:T(8,128)(2,1)S(1)} all-to-all(bf16[256,16,256]{2,1,0:T(8,128)(2,1)S(1)} %copy.29), channel_id=1, replica_groups=mesh['vol'=16,'img'=32] {'vol'}, dimensions={0} | all-to-all | bytes 4194304 | tf_op jit(solution)/shard_map/all_to_all | solution.py:92
  236.9 0.2 copy.30
  237.2 3.1 copy.31
  240.3 0.0 reduce-scatter.5.cloned.1.call-update
  240.3 123.7 %reduce-scatter.5.cloned.1.call-done = bf16[16,256,8]{1,0,2:T(8,128)(2,1)} async-done(((bf16[16,256,256]{1,0,2:T(8,128)(2,1)}), bf16[16,256,8]{1,0,2:T(8,128)(2,1)}) %reduce-scatter.5.cloned.1.call-update) | async-done | bytes 65552 | tf_op jit(solution)/shard_map/reduce_scatter | solution.py:93
  364.1 1.5 copy.32
  (10 shorter events, 0.1 us)
Async XLA Ops:
  7.2 1.6 copy-start
  7.2 70.7 %all-gather.2.cloned.1.call-start = ((), (), s32[]{:S(2)}) async-start(), calls=%async_computation.3 | async-start | bytes 2162688 | tf_op jit(solution)/shard_map/all_gather | solution.py:54
  8.7 136.2 %reduce-scatter.3.cloned.1.call-start = ((), (), s32[]{:S(2)}) async-start(), calls=%async_computation.4 | async-start | bytes 2228224 | tf_op jit(solution)/shard_map/reduce_scatter | solution.py:55
  81.5 282.5 %reduce-scatter.5.cloned.1.call-start = ((), (), s32[]{:S(2)}) async-start(), calls=%async_computation.5 | async-start | bytes 2162688 | tf_op jit(solution)/shard_map/reduce_scatter | solution.py:93
  81.7 6.5 %copy-start.5 = (f32[32]{0:T(128)S(1)}, f32[32]{0:T(128)}, u32[]{:S(2)}) copy-start(f32[32]{0:T(128)} %param.13) | copy-start | bytes 388
  81.7 6.6 %copy-start.2 = (s32[512]{0:T(512)S(1)}, s32[512]{0:T(512)}, u32[]{:S(2)}) copy-start(s32[512]{0:T(512)} %param.14) | copy-start | bytes 6148
  144.9 3.4 copy-start.3
  144.9 53.8 %copy-start.4 = (f32[512]{0:T(512)S(1)}, f32[512]{0:T(512)}, u32[]{:S(2)}) copy-start(f32[512]{0:T(512)} %param.15) | copy-start | bytes 6148
  199.1 8.1 %copy-start.1 = (f32[512,16]{0,1:T(8,128)}, f32[512,16]{0,1:T(8,128)S(1)}, u32[]{:S(2)}) copy-start(f32[512,16]{0,1:T(8,128)S(1)} %fusion.44) | copy-start | bytes 98308
Sparse Core Ops, SparseCore 0:
  11.7 66.1 all-gather.1
  81.7 63.1 reduce-scatter.2
  240.5 123.5 reduce-scatter.4
where the time goes:
time: 374 us; the launch traced here: 372 us
  waiting for transfers between devices  239 us (64%)
  blocking collectives  77.6 us (21%)
  matrix products  23.7 us (6%)
  local copies, waits for them, and re-layouts  17.1 us (5%)
  between operations  13.9 us (4%)
    reduce_scatter x1, waiting for transfers between devices, per_device(): lax.psum_scatter(arrived.astype(jnp.float32).astype(jnp.bfloat16), 'img',...  124 us
    all_gather x1, waiting for transfers between devices, per_device(): full_slab = lax.all_gather(volume, 'img', axis=1, tiled=True)  66.2 us
    reduce_scatter x1, waiting for transfers between devices, per_device(): lax.psum_scatter(jnp.einsum('oyz,zyx->yox', slab_weights, full_slab, pref...  49.2 us
    psum x1, blocking collectives, per_device(): scores, energy = lax.psum((scores, energy), 'vol')  47.8 us
    all_to_all x1, blocking collectives, per_device(): lax.all_to_all(backprojected, 'vol', split_axis=0, concat_axis=1, tiled=T...  29.8 us
    unnamed x16, local copies, waits for them, and re-layouts  9.39 us
  transfers between devices with their start and end apart: 3, of which 3 were waited for; matrix products, arithmetic and copies ran while one was open for 5% of the time, Pallas kernels for 0%

commit v1 on v0

v1 whole, which is shorter than its diff:
```python
import functools
import math

import jax
import jax.numpy as jnp
from jax import lax
from jax.experimental import pallas as pl
from jax.experimental.pallas import tpu as pltpu
from jax.sharding import PartitionSpec as P

phase_offset = math.asin(0.1) / math.pi
epsilon = 1e-05
bf16 = jnp.bfloat16
f32 = jnp.float32
LANES = 128
VMEM = pl.BlockSpec(memory_space=pltpu.VMEM)
SMEM = pl.BlockSpec(memory_space=pltpu.SMEM)


def call(body, out_shape, in_specs, out_specs, scratch=(), grid=(), flops=0, nbytes=0, vmem=48):
    return pl.pallas_call(
        body,
        out_shape=out_shape,
        grid=grid,
        in_specs=in_specs,
        out_specs=out_specs,
        scratch_shapes=list(scratch),
        cost_estimate=pl.CostEstimate(flops=flops, bytes_accessed=nbytes, transcendentals=0),
        compiler_params=pltpu.CompilerParams(vmem_limit_bytes=vmem * 2**20),
    )


def dot(a, b, contract):
    return lax.dot_general(a, b, ((contract[0], contract[1]), ((), ())), preferred_element_type=f32)


def minus_sine_pi(turns):
    whole = jnp.floor(turns + 0.5)
    rest = turns - whole
    odd = whole - 2.0 * jnp.floor(whole * 0.5)
    x = rest * math.pi
    square = x * x
    total = -1.0 / 39916800.0
    for term in (1.0 / 362880.0, -1.0 / 5040.0, 1.0 / 120.0, -1.0 / 6.0, 1.0):
        total = total * square + term
    return total * x * (2.0 * odd - 1.0)


def swap_blocks(parts, stride):
    count = len(parts)
    lane = lax.broadcasted_iota(jnp.int32, parts[0].shape, parts[0].ndim - 1)
    bit = 1
    while bit < count:
        shift = stride * bit
        low = (lane & shift) == 0
        axis = parts[0].ndim - 1
        result = list(parts)
        for i in range(count):
            if i & bit:
                continue
            a, c = parts[i], parts[i | bit]
            result[i] = jnp.where(low, a, pltpu.roll(c, shift, axis))
            result[i | bit] = jnp.where(low, pltpu.roll(a, LANES - shift, axis), c)
        parts = result
        bit *= 2
    return parts


def weigh_body(block, rows, cols, group_total, first_row, defocus, groups, images, out, square, table, spread, square_spread):
    halves = cols // LANES

    @pl.when(pl.program_id(0) == 0)
    def _():
        row = (lax.broadcasted_iota(jnp.int32, (rows, cols), 0) + first_row[0]).astype(f32)
        col = lax.broadcasted_iota(jnp.int32, (rows, cols), 1).astype(f32)
        row_freq = (row - rows * 8.0) * (2.0 / (rows * 16.0))
        col_freq = (col - cols // 2) * (2.0 / cols)
        radius = 0.5 * (row_freq * row_freq + col_freq * col_freq)

        def one(g, _):
            value = minus_sine_pi(radius * defocus[g] + phase_offset)
            table[g] = value
            value = value * value
            for h in range(halves):
                square_spread[h, pl.ds(g, rows, stride=group_total), :] = value[:, h * LANES : (h + 1) * LANES]
            return 0

        lax.fori_loop(0, group_total, one, 0, unroll=4)
        for r in range(rows):
            for h in range(halves):
                value = square_spread[h, r * group_total : (r + 1) * group_total, :]
                high = value.astype(bf16)
                square[r, 0, :, h * LANES : (h + 1) * LANES] = high
                square[r, 1, :, h * LANES : (h + 1) * LANES] = (value - high.astype(f32)).astype(bf16)

    base = pl.program_id(0) * block

    def one(n, _):
        value = images[n].astype(f32) * table[groups[base + n]]
        for h in range(halves):
            spread[h, pl.ds(n, rows, stride=block), :] = value[:, h * LANES : (h + 1) * LANES]
        return 0

    lax.fori_loop(0, block, one, 0, unroll=8)
    for r in range(rows):
        for h in range(halves):
            out[r, :, h * LANES : (h + 1) * LANES] = spread[h, r * block : (r + 1) * block, :].astype(bf16)


def template_body(planes, bins, depth, received, out):
    sources = received.shape[0]
    total = sources * planes
    where = lax.broadcasted_iota(jnp.int32, (bins, total), 1).astype(f32)
    deep = jnp.concatenate([depth[...]] * (total // LANES), axis=1)
    weight = jnp.maximum(0.0, 1.0 - jnp.abs(where - deep)).astype(bf16)
    rows = received[:, :planes, :].reshape(total, LANES)
    chosen = received[:, planes:, :].reshape(-1, LANES)
    table = dot(weight, rows, ((1,), (0,))).astype(bf16)
    empty = jnp.zeros_like(table)
    listed = chosen.shape[0] // sources
    low = dot(chosen, jnp.concatenate([table, empty], axis=0), ((1,), (0,))).astype(bf16)
    high = dot(chosen, jnp.concatenate([empty, table], axis=0), ((1,), (0,))).astype(bf16)
    out[:sources] = low.reshape(sources, listed, LANES)
    out[sources:] = high.reshape(sources, listed, LANES)


def score_body(templates, weighted, square, out, scores, energy):
    step = pl.program_id(0)
    rows = weighted.shape[0]
    total = None
    power = None
    for r in range(rows):
        piece = jnp.concatenate([templates[2 * r], templates[2 * r + 1]], axis=1)
        part = dot(piece, weighted[r], ((1,), (1,)))
        total = part if total is None else total + part
        wide = piece.astype(f32)
        wide = wide * wide
        high = wide.astype(bf16)
        low = (wide - high.astype(f32)).astype(bf16)
        left = jnp.concatenate([high, high, low], axis=1)
        right = jnp.concatenate([square[r, 0], square[r, 1], square[r, 0]], axis=1)
        part = dot(left, right, ((1,), (1,)))
        power = part if power is None else power + part
    group_total = power.shape[1]

    @pl.when(step == 0)
    def _():
        scores[...] = total
        energy[...] = jnp.zeros_like(energy)
        energy[:, :group_total] = power

    @pl.when(step > 0)
    def _():
        scores[...] += total
        energy[:, :group_total] += power

    @pl.when(step == pl.num_programs(0) - 1)
    def _():
        chunks = scores.shape[1] // LANES
        listed = scores.shape[0]
        values = [scores[:, c * LANES : (c + 1) * LANES] for c in range(chunks)]
        tail = energy[: listed // 2] + pltpu.roll(energy[listed // 2 :], group_total, 1)
        for k in range(out.shape[0]):
            for c in range(chunks):
                out[k, c * listed : (c + 1) * listed, :] = values[c]
            out[k, chunks * listed :, :] = tail


def posterior_body(group_total, partial, groups, sharpness, weighted, posteriors, out, rounded):
    step = pl.program_id(0)
    listed = posteriors.shape[0]
    images = posteriors.shape[1]

    @pl.when(step == 0)
    def _():
        summed = partial[0]
        for k in range(1, partial.shape[0]):
            summed = summed + partial[k]
        chunks = images // LANES
        scores = jnp.concatenate([summed[c * listed : (c + 1) * listed] for c in range(chunks)], axis=1)
        scale = 1.0 / jnp.sqrt(summed[chunks * listed :] + epsilon)
        scale = jnp.concatenate([scale, pltpu.roll(scale, LANES - group_total, 1)], axis=0)
        member = lax.broadcasted_iota(jnp.int32, (LANES, images), 0) == groups[...]
        member = member.astype(f32)
        picked = lax.dot_general(
            scale, member, (((1,), (0,)), ((), ())), precision=lax.Precision.HIGHEST, preferred_element_type=f32
        )
        logits = sharpness[...] * scores * picked
        logits = jnp.exp(logits - jnp.max(logits, axis=0, keepdims=True))
        result = logits / jnp.sum(logits, axis=0, keepdims=True)
        posteriors[...] = result
        rounded[...] = result.astype(bf16)

    rows = weighted.shape[0]
    for r in range(rows):
        part = dot(rounded[...], weighted[r], ((1,), (0,)))
        out[r] = part


def spread_body(summed, out):
    rows, listed, cols = summed.shape
    for o in range(0, listed, 8):
        for h in range(cols // LANES):
            parts = [summed[r, o : o + 8, h * LANES : (h + 1) * LANES] for r in range(rows)]
            parts = swap_blocks(parts, LANES // rows)
            for j in range(rows):
                out[h * rows + j, o : o + 8, :] = parts[j].astype(bf16)


def project_body(planes, bins, reach, centre, tilt, chosen, arrived, out):
    sources = chosen.shape[0]
    half = sources * (chosen.shape[1] - planes)
    picker = chosen[:, planes:, :].reshape(half, LANES)
    both = arrived[...].reshape(2 * half, LANES)
    low = dot(both[:half], picker, ((0,), (0,)))
    high = dot(both[half:], picker, ((0,), (0,)))
    lane = lax.broadcasted_iota(jnp.int32, low.shape, 1)
    by_bin = jnp.where(lane < bins, low, high)
    rows = reach.shape[0]
    width = LANES // rows
    parts = []
    lane = lax.broadcasted_iota(jnp.int32, (bins, LANES), 1)
    for r in range(rows):
        deep = centre[...] + tilt[...] * reach[r]
        weights = []
        for h in range(2):
            where = ((lane % 16) * planes + h * 8 + lane // 16).astype(f32)
            weights.append(jnp.maximum(0.0, 1.0 - jnp.abs(where - deep)).astype(bf16))
        weight = jnp.concatenate(weights, axis=1)
        weight = jnp.concatenate([weight, weight], axis=0)
        parts.append(dot(by_bin[r * width : (r + 1) * width].astype(bf16), weight, ((1,), (0,))))
    first = swap_blocks([part[:, :LANES] for part in parts], 1)
    second = swap_blocks([part[:, LANES:] for part in parts], 1)
    for j in range(rows):
        out[j] = jnp.concatenate([first[j], second[j]], axis=0).astype(bf16)


def final_body(arrived, out):
    bands = arrived.shape[0]
    wide = arrived[...].astype(f32)
    for zh in range(2):
        for vh in range(bands // 8):
            parts = [wide[vh * 8 + k, zh * 8 : (zh + 1) * 8, :] for k in range(8)]
            parts = swap_blocks(parts, LANES // 8)
            for zl in range(8):
                out[zh * 8 + zl, :, vh * LANES : (vh + 1) * LANES] = parts[zl]


def per_device(volume, images, bin_lists, bin_planes, bin_tilts, defocus, groups, precision):
    bands = lax.axis_size("vol")
    blocks = lax.axis_size("img")
    half_group = blocks // 2
    planes, strip, cols = volume.shape
    image_count, rows, _ = images.shape
    height = rows * bands
    bins = bin_planes.shape[0]
    listed = bin_lists.shape[1]
    group_total = defocus.shape[0]
    lane_halves = cols // LANES
    vol_index = lax.axis_index("vol")
    img_index = lax.axis_index("img")
    halves = [list(range(half_group)), list(range(half_group, blocks))]

    sent = volume.reshape(planes, strip, lane_halves, LANES).transpose(1, 2, 0, 3)
    sent = sent.reshape(strip * lane_halves, planes, LANES)
    route = [
        (v * blocks + i, (i // 2) * blocks + (i % 2) * half_group + v)
        for v in range(bands)
        for i in range(blocks)
    ]
    moved = lax.ppermute(sent, ("vol", "img"), route)

    other = lax.ppermute(bin_lists, "img", [(i, (i + half_group) % blocks) for i in range(blocks)])
    upper = img_index >= half_group
    low_list = jnp.where(upper, other[0], bin_lists[0])
    high_list = jnp.where(upper, bin_lists[0], other[0])
    lane_ids = jnp.arange(2 * bins)[None, :]
    chosen = (lane_ids == low_list[:, None]) | (lane_ids == high_list[:, None] + bins)
    chosen = chosen.astype(bf16)

    first_row = vol_index * rows
    own_row = first_row + img_index // 2

    def reach_of(ids):
        return float(planes) * ((ids.astype(f32) - (height - 1) * 0.5) * (2.0 / height))

    centre = jnp.broadcast_to(bin_planes.astype(f32)[:, None], (bins, LANES))
    tilt = jnp.broadcast_to(bin_tilts[:, None], (bins, LANES))
    depth = centre + tilt * reach_of(own_row)
    reach = reach_of(first_row + jnp.arange(rows))

    block = 64
    weighted, square = call(
        functools.partial(weigh_body, block, rows, cols, group_total),
        (
            jax.ShapeDtypeStruct((rows, image_count, cols), bf16),
            jax.ShapeDtypeStruct((rows, 2, group_total, cols), bf16),
        ),
        [SMEM, SMEM, SMEM, pl.BlockSpec((block, rows, cols), lambda i: (i, 0, 0))],
        (
            pl.BlockSpec((rows, block, cols), lambda i: (0, i, 0)),
            pl.BlockSpec((rows, 2, group_total, cols), lambda i: (0, 0, 0, 0)),
        ),
        scratch=(
            pltpu.VMEM((group_total, rows, cols), f32),
            pltpu.VMEM((lane_halves, rows * block, LANES), f32),
            pltpu.VMEM((lane_halves, rows * group_total, LANES), f32),
        ),
        grid=(image_count // block,),
        flops=40 * image_count * rows * cols,
        nbytes=4 * image_count * rows * cols,
    )(first_row.reshape(1), defocus, groups, images)

    packed = jnp.concatenate(
        [moved, jnp.broadcast_to(chosen[None], (half_group,) + chosen.shape)], axis=1
    )
    gathered = lax.all_to_all(packed, "img", 0, 0, tiled=True, axis_index_groups=halves)
    pieces = call(
        functools.partial(template_body, planes, bins),
        jax.ShapeDtypeStruct((blocks, listed, LANES), bf16),
        [VMEM, VMEM],
        VMEM,
    )(depth, gathered)
    templates = lax.all_to_all(pieces, "img", 0, 0, tiled=True)

    step_rows = 4
    payload_rows = listed * (image_count // LANES) + listed // 2
    partial = call(
        score_body,
        jax.ShapeDtypeStruct((bands, payload_rows, LANES), f32),
        [
            pl.BlockSpec((step_rows * lane_halves, listed, LANES), lambda i: (i, 0, 0)),
            pl.BlockSpec((step_rows, image_count, cols), lambda i: (i, 0, 0)),
            pl.BlockSpec((step_rows, 2, group_total, cols), lambda i: (i, 0, 0, 0)),
        ],
        pl.BlockSpec((bands, payload_rows, LANES), lambda i: (0, 0, 0)),
        scratch=(pltpu.VMEM((listed, image_count), f32), pltpu.VMEM((listed, LANES), f32)),
        grid=(rows // step_rows,),
    )(templates, weighted, square)
    partial = lax.all_to_all(partial, "vol", 0, 0, tiled=True)

    posteriors, summed = call(
        functools.partial(posterior_body, group_total),
        (
            jax.ShapeDtypeStruct((listed, image_count), f32),
            jax.ShapeDtypeStruct((rows, listed, cols), f32),
        ),
        [
            VMEM_BLOCK((bands, payload_rows, LANES)),
            VMEM_BLOCK((1, image_count)),
            VMEM_BLOCK((1, image_count)),
            pl.BlockSpec((step_rows, image_count, cols), lambda i: (i, 0, 0)),
        ],
        (
            VMEM_BLOCK((listed, image_count)),
            pl.BlockSpec((step_rows, listed, cols), lambda i: (i, 0, 0)),
        ),
        scratch=(pltpu.VMEM((listed, image_count), bf16),),
        grid=(rows // step_rows,),
    )(partial, groups.reshape(1, image_count), precision.reshape(1, image_count), weighted)
    spread = call(
        spread_body,
        jax.ShapeDtypeStruct((blocks, listed, LANES), bf16),
        [VMEM],
        VMEM,
    )(summed)
    arrived = lax.all_to_all(spread, "img", 0, 0, tiled=True)

    projected = call(
        functools.partial(project_body, planes, bins),
        jax.ShapeDtypeStruct((bands, planes, LANES), bf16),
        [SMEM, VMEM, VMEM, VMEM, VMEM],
        VMEM,
    )(reach, centre, tilt, gathered, arrived)
    slabs = lax.all_to_all(projected, "vol", 0, 0, tiled=True)
    numerator = call(
        final_body,
        jax.ShapeDtypeStruct((planes, cols // blocks, height), f32),
        [VMEM],
        VMEM,
    )(slabs)
    return (posteriors.T, numerator.transpose(0, 2, 1))


def VMEM_BLOCK(shape):
    return pl.BlockSpec(shape, lambda i: (0,) * len(shape))


def solution(mesh):
    placed = (
        P("vol", "img", None),
        P("img", "vol", None),
        P("img", None),
        P(),
        P(),
        P(),
        P("img"),
        P("img"),
    )
    return jax.shard_map(
        per_device,
        mesh=mesh,
        in_specs=placed,
        out_specs=(P("img", None), P("vol", None, "img")),
        check_vma=False,
    )
```

time: 374 us -> 134 us (0.36)
  waiting for transfers between devices: 239 us -> 17.9 us
  starting transfers between devices: 0.12 us -> 49.2 us
  blocking collectives: 77.6 us -> 37.6 us
  matrix products: 23.7 us -> 0 us
  Pallas kernels: 0 us -> 19.2 us
  between operations: 13.9 us -> 0.76 us
  local copies, waits for them, and re-layouts: 17.1 us -> 6.58 us
    reduce_scatter x2 -> x0, waiting for transfers between devices: 173 us -> none  [the longest x1 124 us: per_device(): lax.psum_scatter(arrived.astype(jnp.float32).astype(jnp.bfloat16), 'img',...]
    all_gather x1 -> x0, waiting for transfers between devices: 66.2 us -> none  [per_device(): full_slab = lax.all_gather(volume, 'img', axis=1, tiled=True)]
    psum x1 -> x0, blocking collectives: 47.8 us -> none  [per_device(): scores, energy = lax.psum((scores, energy), 'vol')]
    all_to_all x0 -> x3, starting transfers between devices: none -> 33 us  [the longest x1 16.3 us: per_device(): lax.all_to_all(packed, 'img', 0, 0, tiled=True, axis_index_groups=halves)]
    dot_general x8 -> x0, matrix products: 23.7 us -> none  [the longest x1 7.36 us: per_device(): jnp.dot(member, ctf_rows.reshape(group_total, band_rows * col_count), pre...]
    pallas_call x0 -> x7, Pallas kernels: none -> 19.2 us  [the longest x1 11.3 us: per_device(): call(functools.partial(weigh_body, block, rows, cols, group_total), (jax....]
    all_to_all x0 -> x3, waiting for transfers between devices: none -> 17.3 us  [the longest x1 10.9 us: per_device(): arrived = lax.all_to_all(spread, 'img', 0, 0, tiled=True)]
    ppermute x0 -> x2, starting transfers between devices: none -> 16.2 us  [the longest x1 11.5 us: per_device(): lax.ppermute(bin_lists, 'img', [(i, (i + half_group) % blocks) for i in r...]
  transfers between devices with their start and end apart: 3 -> 5, of which waited for: 3 -> 3; matrix products, arithmetic and copies ran while one was open for 5% -> 2% of each run, Pallas kernels for 0% -> 9%
where the time goes in v1:
time: 134 us; the launch traced here: 133 us
  starting transfers between devices  49.2 us (37%)
  blocking collectives  37.6 us (28%)
  Pallas kernels  19.2 us (14%)
  waiting for transfers between devices  17.9 us (13%)
  local copies, waits for them, and re-layouts  6.58 us (5%)
  other arithmetic  2.09 us (2%)
    all_to_all x1, blocking collectives, per_device(): partial = lax.all_to_all(partial, 'vol', 0, 0, tiled=True)  27.5 us
    all_to_all x1, starting transfers between devices, per_device(): lax.all_to_all(packed, 'img', 0, 0, tiled=True, axis_index_groups=halves)  16.3 us
    all_to_all x1, starting transfers between devices, per_device(): arrived = lax.all_to_all(spread, 'img', 0, 0, tiled=True)  11.9 us
    ppermute x1, starting transfers between devices, per_device(): lax.ppermute(bin_lists, 'img', [(i, (i + half_group) % blocks) for i in r...  11.5 us
    pallas_call x1, Pallas kernels, per_device(): call(functools.partial(weigh_body, block, rows, cols, group_total), (jax....  11.3 us
    all_to_all x1, waiting for transfers between devices, per_device(): arrived = lax.all_to_all(spread, 'img', 0, 0, tiled=True)  10.9 us
    all_to_all x1, blocking collectives, per_device(): slabs = lax.all_to_all(projected, 'vol', 0, 0, tiled=True)  10.1 us
    all_to_all x1, waiting for transfers between devices, per_device(): lax.all_to_all(packed, 'img', 0, 0, tiled=True, axis_index_groups=halves)  6.37 us
  transfers between devices with their start and end apart: 5, of which 3 were waited for; matrix products, arithmetic and copies ran while one was open for 2% of the time, Pallas kernels for 9%

profile of v1, /device:TPU:1, one launch (start us, length us, event | category | flops | bytes accessed | tf_op | source)
XLA Modules:
  0.0 133.2 jit_solution(9078362242953530892)
XLA Ops:
  0.6 11.5 %collective-permute-start.1 = (s32[1,16]{1,0:T(1,128)}, s32[1,16]{1,0:T(1,128)S(1)}, u32[]{:S(2)}, u32[]{:S(2)}) collective-permute-start(s32[1,16]{1,0:T(1,128)} %param.10), channel_id=1, source_target_pairs={{0,16},{1,17},{2,18},{3,19},{4,20},{5,21},{6,22},{7,23},{8,24},{9,... | collective-permute-start | bytes 200 | tf_op jit(solution)/shard_map/ppermute | solution.py:273
  12.1 0.9 copy.10
  13.0 4.8 %collective-permute-start = (bf16[16,16,128]{2,1,0:T(8,128)(2,1)S(1)}, bf16[16,16,128]{2,1,0:T(8,128)(2,1)S(1)}, u32[]{:S(2)}, u32[]{:S(2)}) collective-permute-start(bf16[16,16,128]{2,1,0:T(8,128)(2,1)S(1)} %bitcast.17), channel_id=1, source_target_pairs={{0,0},{1,16},{2,32},{3,48},{4,64},{5,80},{6,96},{7,112},{8,128},{9... | collective-permute-start | bytes 196616 | tf_op jit(solution)/shard_map/ppermute | solution.py:271
  17.7 0.0 collective-permute-done.1
  17.8 0.7 fusion.2
  18.4 0.1 fusion.1
  18.5 0.6 collective-permute-done
  19.1 0.7 pad_maximum_fusion
  19.7 16.3 %all-to-all-start = ((bf16[16,32,128]{2,1,0:T(8,128)(2,1)}), bf16[16,32,128]{2,1,0:T(8,128)(2,1)S(1)}, u32[]{:S(2)}, u32[]{:S(2)}) async-start(bf16[16,32,128]{2,1,0:T(8,128)(2,1)} %pad_maximum_fusion), calls=%async_computation | async-start | bytes 262144 | tf_op jit(solution)/shard_map/all_to_all | solution.py:317
  36.0 0.7 multiply_add_fusion
  36.7 6.4 %all-to-all-done.received.chosen = bf16[16,32,128]{2,1,0:T(8,128)(2,1)S(1)} async-done(((bf16[16,32,128]{2,1,0:T(8,128)(2,1)}), bf16[16,32,128]{2,1,0:T(8,128)(2,1)S(1)}, u32[]{:S(2)}, u32[]{:S(2)}) %all-to-all-start) | async-done | bytes 131104 | tf_op jit(solution)/shard_map/all_to_all | solution.py:317
  43.1 0.1 broadcast_in_dim.8.depth
  43.2 1.0 shard_map.95
  44.1 4.8 %all-to-all-start.1 = ((bf16[32,16,128]{2,1,0:T(8,128)(2,1)}), bf16[32,16,128]{2,1,0:T(8,128)(2,1)S(1)}, u32[]{:S(2)}, u32[]{:S(2)}) async-start(bf16[32,16,128]{2,1,0:T(8,128)(2,1)} %shard_map.95), calls=%async_computation.1 | async-start | bytes 262144 | tf_op jit(solution)/shard_map/all_to_all | solution.py:324
  48.9 0.0 copy-start.3
  48.9 0.7 copy-done.3
  49.6 0.0 copy-start.6
  49.6 0.7 copy-done.6
  50.2 0.0 copy-start.5
  50.2 11.3 %shard_map.96 = (bf16[16,512,256]{2,1,0:T(8,128)(2,1)S(1)}, bf16[16,2,32,256]{3,2,1,0:T(8,128)(2,1)S(1)}) custom-call(s32[1]{0:T(128)} %bitcast.5.first_row, f32[32]{0:T(128)S(1)} %copy-done.6, s32[512]{0:T(512)S(1)} %copy-done.3, bf16[512,16,256]{2,1,0:T(8,128)(2,1)} %images.1), custom_call_target="tpu_custom_call" | custom-call | flops 83886080 | bytes 8388608 | tf_op jit(solution)/shard_map/pallas_call | solution.py:293
  61.6 0.0 copy-start
  61.6 1.9 %copy-done = bf16[16,512,256]{2,1,0:T(8,128)(2,1)} copy-done((bf16[16,512,256]{2,1,0:T(8,128)(2,1)}, bf16[16,512,256]{2,1,0:T(8,128)(2,1)S(1)}, u32[]{:S(2)}) %copy-start) | copy-done | bytes 4194328
  63.5 0.0 copy-start.4
  63.6 0.0 all-to-all-done.1.templates
  63.6 0.0 copy-start.1
  63.6 2.2 %copy-done.1 = bf16[16,512,256]{2,1,0:T(8,128)(2,1)S(1)} copy-done((bf16[16,512,256]{2,1,0:T(8,128)(2,1)S(1)}, bf16[16,512,256]{2,1,0:T(8,128)(2,1)}, u32[]{:S(2)}) %copy-start.1) | copy-done | bytes 4194328
  65.8 0.0 copy-start.2
  65.8 1.9 %shard_map.97 = f32[16,72,128]{2,1,0:T(8,128)S(1)} custom-call(bf16[32,16,128]{2,1,0:T(8,128)(2,1)S(1)} %all-to-all-done.1.templates, bf16[16,512,256]{2,1,0:T(8,128)(2,1)S(1)} %copy-done.1, bf16[16,2,32,256]{3,2,1,0:T(8,128)(2,1)S(1)} %get-tuple-element.7.square), custom_call_target="tpu_custom_call" | custom-call | tf_op jit(solution)/shard_map/pallas_call | solution.py:328
  67.7 0.0 copy-start.8
  67.7 0.0 copy-start.7
  67.7 27.5 %all_to_all.25.partial = f32[16,72,128]{2,1,0:T(8,128)S(1)} all-to-all(f32[16,72,128]{2,1,0:T(8,128)S(1)} %shard_map.97), channel_id=1, replica_groups=mesh['vol'=16,'img'=32] {'vol'}, dimensions={0} | all-to-all | bytes 1179648 | tf_op jit(solution)/shard_map/all_to_all | solution.py:340
  95.2 0.0 copy-done.5
  95.2 0.0 copy-done.4
  95.2 0.0 copy-done.2
  95.2 1.8 %shard_map.98 = (f32[16,512]{1,0:T(8,128)}, f32[16,16,256]{2,1,0:T(8,128)S(1)}) custom-call(f32[16,72,128]{2,1,0:T(8,128)S(1)} %all_to_all.25.partial, s32[1,512]{1,0:T(1,128)S(1)} %bitcast.13, f32[1,512]{1,0:T(1,128)S(1)} %bitcast.14, bf16[16,512,256]{2,1,0:T(8,128)(2,1)S(1)} %copy-done.2), custom_call_target="tpu_custom_call" | custom-call | tf_op jit(solution)/shard_map/pallas_call | solution.py:342
  97.0 1.0 shard_map.99
  98.0 11.9 %all-to-all-start.3 = ((bf16[32,16,128]{2,1,0:T(8,128)(2,1)}), bf16[32,16,128]{2,1,0:T(8,128)(2,1)S(1)}, u32[]{:S(2)}, u32[]{:S(2)}) async-start(bf16[32,16,128]{2,1,0:T(8,128)(2,1)} %shard_map.99), calls=%async_computation.3 | async-start | bytes 262144 | tf_op jit(solution)/shard_map/all_to_all | solution.py:367
  109.9 0.0 copy-done.8
  109.9 10.9 %all-to-all-done.3.arrived = bf16[32,16,128]{2,1,0:T(8,128)(2,1)S(1)} async-done(((bf16[32,16,128]{2,1,0:T(8,128)(2,1)}), bf16[32,16,128]{2,1,0:T(8,128)(2,1)S(1)}, u32[]{:S(2)}, u32[]{:S(2)}) %all-to-all-start.3) | async-done | bytes 131104 | tf_op jit(solution)/shard_map/all_to_all | solution.py:367
  120.9 0.1 broadcast_in_dim.10.centre
  120.9 0.0 copy-done.7
  121.0 0.1 broadcast_in_dim.11.tilt
  121.0 1.3 shard_map.100
  122.3 10.1 %all_to_all.26.arrived = bf16[16,16,128]{2,1,0:T(8,128)(2,1)S(1)} all-to-all(bf16[16,16,128]{2,1,0:T(8,128)(2,1)S(1)} %shard_map.100), channel_id=1, replica_groups=mesh['vol'=16,'img'=32] {'vol'}, dimensions={0} | all-to-all | bytes 131072 | tf_op jit(solution)/shard_map/all_to_all | solution.py:375
  132.4 0.9 shard_map.101
  (3 shorter events, 0.0 us)
Async XLA Ops:
  0.6 17.1 %collective-permute-start.1 = (s32[1,16]{1,0:T(1,128)}, s32[1,16]{1,0:T(1,128)S(1)}, u32[]{:S(2)}, u32[]{:S(2)}) collective-permute-start(s32[1,16]{1,0:T(1,128)} %param.10), channel_id=1, source_target_pairs={{0,16},{1,17},{2,18},{3,19},{4,20},{5,21},{6,22},{7,23},{8,24},{9,... | collective-permute-start | bytes 200 | tf_op jit(solution)/shard_map/ppermute | solution.py:273
  13.0 6.1 %collective-permute-start = (bf16[16,16,128]{2,1,0:T(8,128)(2,1)S(1)}, bf16[16,16,128]{2,1,0:T(8,128)(2,1)S(1)}, u32[]{:S(2)}, u32[]{:S(2)}) collective-permute-start(bf16[16,16,128]{2,1,0:T(8,128)(2,1)S(1)} %bitcast.17), channel_id=1, source_target_pairs={{0,0},{1,16},{2,32},{3,48},{4,64},{5,80},{6,96},{7,112},{8,128},{9... | collective-permute-start | bytes 196616 | tf_op jit(solution)/shard_map/ppermute | solution.py:271
  19.7 23.4 %all-to-all-start = ((bf16[16,32,128]{2,1,0:T(8,128)(2,1)}), bf16[16,32,128]{2,1,0:T(8,128)(2,1)S(1)}, u32[]{:S(2)}, u32[]{:S(2)}) async-start(bf16[16,32,128]{2,1,0:T(8,128)(2,1)} %pad_maximum_fusion), calls=%async_computation | async-start | bytes 262144 | tf_op jit(solution)/shard_map/all_to_all | solution.py:317
  44.1 19.4 %all-to-all-start.1 = ((bf16[32,16,128]{2,1,0:T(8,128)(2,1)}), bf16[32,16,128]{2,1,0:T(8,128)(2,1)S(1)}, u32[]{:S(2)}, u32[]{:S(2)}) async-start(bf16[32,16,128]{2,1,0:T(8,128)(2,1)} %shard_map.95), calls=%async_computation.1 | async-start | bytes 262144 | tf_op jit(solution)/shard_map/all_to_all | solution.py:324
  48.9 0.7 copy-start.3
  49.6 0.7 copy-start.6
  50.2 44.9 %copy-start.5 = (f32[512]{0:T(512)S(1)}, f32[512]{0:T(512)}, u32[]{:S(2)}) copy-start(f32[512]{0:T(512)} %param.15) | copy-start | bytes 6148
  61.6 2.0 %copy-start = (bf16[16,512,256]{2,1,0:T(8,128)(2,1)}, bf16[16,512,256]{2,1,0:T(8,128)(2,1)S(1)}, u32[]{:S(2)}) copy-start(bf16[16,512,256]{2,1,0:T(8,128)(2,1)S(1)} %get-tuple-element.6.weighted) | copy-start | bytes 12582916
  63.5 31.6 %copy-start.4 = (s32[512]{0:T(512)S(1)}, s32[512]{0:T(512)}, u32[]{:S(2)}) copy-start(s32[512]{0:T(512)} %groups.1) | copy-start | bytes 6148
  63.6 2.2 %copy-start.1 = (bf16[16,512,256]{2,1,0:T(8,128)(2,1)S(1)}, bf16[16,512,256]{2,1,0:T(8,128)(2,1)}, u32[]{:S(2)}) copy-start(bf16[16,512,256]{2,1,0:T(8,128)(2,1)} %copy-done) | copy-start | bytes 12582916
  65.8 29.4 %copy-start.2 = (bf16[16,512,256]{2,1,0:T(8,128)(2,1)S(1)}, bf16[16,512,256]{2,1,0:T(8,128)(2,1)}, u32[]{:S(2)}) copy-start(bf16[16,512,256]{2,1,0:T(8,128)(2,1)} %copy-done) | copy-start | bytes 12582916
  67.7 42.3 %copy-start.8 = (s32[64]{0:T(128)S(1)}, s32[64]{0:T(128)}, u32[]{:S(2)}) copy-start(s32[64]{0:T(128)} %param.11) | copy-start | bytes 772
  67.7 53.3 %copy-start.7 = (f32[64]{0:T(128)S(1)}, f32[64]{0:T(128)}, u32[]{:S(2)}) copy-start(f32[64]{0:T(128)} %param.12) | copy-start | bytes 772
  98.0 22.9 %all-to-all-start.3 = ((bf16[32,16,128]{2,1,0:T(8,128)(2,1)}), bf16[32,16,128]{2,1,0:T(8,128)(2,1)S(1)}, u32[]{:S(2)}, u32[]{:S(2)}) async-start(bf16[32,16,128]{2,1,0:T(8,128)(2,1)} %shard_map.99), calls=%async_computation.3 | async-start | bytes 262144 | tf_op jit(solution)/shard_map/all_to_all | solution.py:367

commit v2 on v1

v2 whole, which is shorter than its diff:
```python
import functools
import math

import jax
import jax.numpy as jnp
from jax import lax
from jax.experimental import pallas as pl
from jax.experimental.pallas import tpu as pltpu
from jax.sharding import PartitionSpec as P

phase_offset = math.asin(0.1) / math.pi
epsilon = 1e-05
bf16 = jnp.bfloat16
f32 = jnp.float32
LANES = 128
VMEM = pl.BlockSpec(memory_space=pltpu.VMEM)
SMEM = pl.BlockSpec(memory_space=pltpu.SMEM)


def call(body, out_shape, in_specs, out_specs, scratch=(), grid=(), flops=0, nbytes=0, vmem=16):
    return pl.pallas_call(
        body,
        out_shape=out_shape,
        grid=grid,
        in_specs=in_specs,
        out_specs=out_specs,
        scratch_shapes=list(scratch),
        cost_estimate=pl.CostEstimate(flops=flops, bytes_accessed=nbytes, transcendentals=0),
        compiler_params=pltpu.CompilerParams(vmem_limit_bytes=vmem * 2**20),
    )


def in_hbm(*arrays):
    return [pltpu.with_memory_space_constraint(array, pltpu.HBM) for array in arrays]


def dot(a, b, contract):
    return lax.dot_general(a, b, ((contract[0], contract[1]), ((), ())), preferred_element_type=f32)


def minus_sine_pi(turns):
    whole = jnp.floor(turns + 0.5)
    rest = turns - whole
    odd = whole - 2.0 * jnp.floor(whole * 0.5)
    x = rest * math.pi
    square = x * x
    total = -1.0 / 39916800.0
    for term in (1.0 / 362880.0, -1.0 / 5040.0, 1.0 / 120.0, -1.0 / 6.0, 1.0):
        total = total * square + term
    return total * x * (2.0 * odd - 1.0)


def swap_blocks(parts, stride):
    count = len(parts)
    lane = lax.broadcasted_iota(jnp.int32, parts[0].shape, parts[0].ndim - 1)
    bit = 1
    while bit < count:
        shift = stride * bit
        low = (lane & shift) == 0
        axis = parts[0].ndim - 1
        result = list(parts)
        for i in range(count):
            if i & bit:
                continue
            a, c = parts[i], parts[i | bit]
            result[i] = jnp.where(low, a, pltpu.roll(c, shift, axis))
            result[i | bit] = jnp.where(low, pltpu.roll(a, LANES - shift, axis), c)
        parts = result
        bit *= 2
    return parts


def row_of(rows):
    return lax.axis_index("vol") * rows


def reach_of(row, planes, height):
    return float(planes) * ((row.astype(f32) - (height - 1) * 0.5) * (2.0 / height))


def one_hot(mask):
    return mask.astype(f32).astype(bf16)


def part_body(lists, volume, out):
    planes, strip, cols = volume.shape
    size = planes * strip
    here = lax.broadcasted_iota(jnp.int32, (size, size), 0)
    there = lax.broadcasted_iota(jnp.int32, (size, size), 1)
    mixer = one_hot((here % planes) * strip + here // planes == there)
    mixed = dot(mixer, volume[...].astype(f32).reshape(size, cols).astype(bf16), ((1,), (0,)))
    place = lax.broadcasted_iota(jnp.int32, (planes, LANES), 0)
    lane = lax.broadcasted_iota(jnp.int32, (planes, LANES), 1)
    half = LANES // 2
    hit = (place == 0) & (lane == lists[0] + half)
    for o in range(1, planes):
        hit = hit | ((place == o) & (lane == lists[o] + half))
    listed = hit.astype(f32)
    for h in range(cols // LANES):
        parts = [mixed[r * planes : (r + 1) * planes, h * LANES : (h + 1) * LANES] for r in range(strip)]
        parts = swap_blocks(parts, half // strip)
        for j in range(strip):
            piece = parts[j]
            out[h * 2 * strip + j] = jnp.where(lane < half, piece, listed).astype(bf16)
            out[h * 2 * strip + strip + j] = jnp.where(lane < half, pltpu.roll(piece, half, 1), listed).astype(bf16)


def weigh_body(block, first_row, defocus, groups, bin_planes, bin_tilts, images, out, square, centre, tilt, table, mixer, held, power):
    _, rows, cols = images.shape
    group_total = table.shape[0]

    @pl.when(pl.program_id(0) == 0)
    def _():
        row = (lax.broadcasted_iota(jnp.int32, (rows, cols), 0) + first_row[0]).astype(f32)
        col = lax.broadcasted_iota(jnp.int32, (rows, cols), 1).astype(f32)
        row_freq = (row - cols // 2) * (2.0 / cols)
        col_freq = (col - cols // 2) * (2.0 / cols)
        radius = 0.5 * (row_freq * row_freq + col_freq * col_freq)

        def one(g, _):
            value = minus_sine_pi(radius * defocus[g] + phase_offset)
            table[g] = value
            value = value * value
            high = value.astype(bf16)
            power[0, g] = high
            power[1, g] = (value - high.astype(f32)).astype(bf16)
            return 0

        lax.fori_loop(0, group_total, one, 0, unroll=4)
        size = mixer.shape[0]
        here = lax.broadcasted_iota(jnp.int32, (size, size), 0)
        there = lax.broadcasted_iota(jnp.int32, (size, size), 1)
        mixer[...] = one_hot((here % rows) * rows + here // rows == there)
        for part in range(2):
            for g in range(0, group_total, rows):
                mixed = dot(mixer[...], power[part, g : g + rows].reshape(rows * rows, cols), ((1,), (0,)))
                square[:, part, g : g + rows, :] = mixed.astype(bf16).reshape(rows, rows, cols)
        for q in range(centre.shape[0]):
            centre[q : q + 1, :] = jnp.full((1, LANES), bin_planes[q].astype(f32))
            tilt[q : q + 1, :] = jnp.full((1, LANES), bin_tilts[q])

    base = pl.program_id(0) * block

    def some(k, _):
        for m in range(rows):
            n = k * rows + m
            held[m] = (images[n].astype(f32) * table[groups[base + n]]).astype(bf16)
        mixed = dot(mixer[...], held[...].reshape(rows * rows, cols), ((1,), (0,)))
        out[:, pl.ds(k * rows, rows), :] = mixed.astype(bf16).reshape(rows, rows, cols)
        return 0

    lax.fori_loop(0, block // rows, some, 0, unroll=True)


def band_body(received, after, out):
    lane = lax.broadcasted_iota(jnp.int32, received.shape[1:], 1)
    half = LANES // 2
    for w in range(out.shape[0]):
        first = received[2 * w].astype(f32)
        second = pltpu.roll(received[2 * w + 1].astype(f32), half, 1)
        out[w] = jnp.where(lane < half, first, second).astype(bf16)


def template_body(rows, height, first_row, centre, tilt, received, planes, out):
    bands, slab, _ = planes.shape
    bins = centre.shape[0]
    total = bands * slab
    where = lax.broadcasted_iota(jnp.int32, (bins, total), 1).astype(f32)
    weights = []
    for r in range(rows):
        deep = centre[...] + tilt[...] * reach_of(first_row[0] + r, slab, height)
        deep = jnp.concatenate([deep] * (total // LANES), axis=1)
        weights.append(jnp.maximum(0.0, 1.0 - jnp.abs(where - deep)).astype(bf16))
    every = dot(jnp.concatenate(weights, axis=0), planes[...].reshape(total, LANES), ((1,), (0,)))
    lane = lax.broadcasted_iota(jnp.int32, (bins, LANES), 1)
    table = every[:bins]
    for r in range(1, rows):
        table = jnp.where(lane // (LANES // rows) == r, every[r * bins : (r + 1) * bins], table)
    table = jnp.concatenate([jnp.zeros((LANES - bins, LANES), bf16), table.astype(bf16)], axis=0)
    chosen = received[...].reshape(-1, LANES)
    out[...] = dot(chosen, table, ((1,), (0,))).astype(bf16).reshape(out.shape)


top = 32767.0


def level_code(largest):
    code = jnp.floor(256.0 * jnp.log2(jnp.maximum(largest, 1e-30))) + 2.0
    return code, jnp.exp2(code * (-1.0 / 256.0))


def level_of(code):
    return jnp.exp2(code * (1.0 / 256.0))


def diagonal(count):
    shape = (count, LANES)
    return lax.broadcasted_iota(jnp.int32, shape, 0) == lax.broadcasted_iota(jnp.int32, shape, 1)


def score_body(templates, weighted, square, out, extra):
    rows, images, cols = weighted.shape
    group_total = square.shape[0]
    listed = templates.shape[1]
    total = None
    power = None
    halves = []
    for h in range(cols // LANES):
        parts = [templates[h * rows + j].astype(f32) for j in range(rows)]
        halves.append(swap_blocks(parts, LANES // rows))
    for r in range(rows):
        piece = jnp.concatenate([half[r] for half in halves], axis=1).astype(bf16)
        part = dot(piece, weighted[r], ((1,), (1,)))
        total = part if total is None else total + part
        wide = piece.astype(f32)
        wide = wide * wide
        high = wide.astype(bf16)
        low = (wide - high.astype(f32)).astype(bf16)
        left = jnp.concatenate([high, high, low], axis=1)
        right = jnp.concatenate([square[r, 0], square[r, 1], square[r, 0]], axis=1)
        part = dot(left, right, ((1,), (1,)))
        power = part if power is None else power + part
    group_total = power.shape[1]
    extra[...] = jnp.zeros_like(extra)
    extra[:, :group_total] = power
    power = jnp.maximum(extra[...], 0.0)
    row_code, row_scale = level_code(jnp.max(jnp.abs(total), axis=1, keepdims=True))
    total = total * row_scale
    image_code, image_scale = level_code(jnp.max(jnp.abs(total), axis=0, keepdims=True))
    total = jnp.clip(jnp.floor(total * image_scale * top + 0.5), -top, top)
    power_code, power_scale = level_code(jnp.max(power, axis=1, keepdims=True))
    power = jnp.minimum(power * power_scale, 1.0) * top
    high = jnp.floor(power)
    low = jnp.floor((power - high) * top + 0.5)
    half = listed // 2
    extra[:half] = (
        high[:half]
        + pltpu.roll(high[half:], group_total, 1)
        + pltpu.roll(low[:half], 2 * group_total, 1)
        + pltpu.roll(low[half:], 3 * group_total, 1)
    )
    chunks = images // LANES
    for c in range(chunks):
        extra[half + c : half + c + 1, :] = image_code[:, c * LANES : (c + 1) * LANES]
    square_mask = diagonal(listed)
    for place, code in ((half + chunks, row_code), (half + chunks + 1, power_code)):
        extra[place : place + 1, :] = jnp.sum(jnp.where(square_mask, code, 0.0), axis=0, keepdims=True)
    extra[half + chunks + 2 :, :] = jnp.zeros((listed - half - chunks - 2, LANES), f32)
    pieces = [total[:, c * LANES : (c + 1) * LANES] for c in range(chunks)] + [extra[...]]
    pieces = [piece.astype(jnp.int32).astype(jnp.int16) for piece in pieces]
    for k in range(out.shape[0]):
        for c, piece in enumerate(pieces):
            out[k, c * listed : (c + 1) * listed, :] = piece


def posterior_body(group_total, partial, groups, sharpness, weighted, posteriors, out):
    listed, images = posteriors.shape
    rows, _, cols = weighted.shape
    chunks = images // LANES
    half = listed // 2
    square_mask = diagonal(listed)
    lane = lax.broadcasted_iota(jnp.int32, (half, LANES), 1)
    scores = None
    power = None
    for k in range(partial.shape[0]):
        value = partial[k].astype(jnp.int32).astype(f32)
        extra = value[chunks * listed :]
        row_level, power_level = (
            level_of(jnp.sum(jnp.where(square_mask, extra[place : place + 1], 0.0), axis=1, keepdims=True)) / top
            for place in (half + chunks, half + chunks + 1)
        )
        image_level = [level_of(extra[half + c : half + c + 1]) for c in range(chunks)]
        part = [value[c * listed : (c + 1) * listed] * row_level * image_level[c] for c in range(chunks)]
        scores = part if scores is None else [a + b for a, b in zip(scores, part)]
        part = extra[:half] + pltpu.roll(extra[:half], LANES - 2 * group_total, 1) * (1.0 / top)
        part = part * jnp.where(lane < group_total, power_level[:half], power_level[half:])
        power = part if power is None else power + part
    scores = jnp.concatenate(scores, axis=1)
    power = jnp.where(lane < 2 * group_total, power, 0.0)
    scale = 1.0 / jnp.sqrt(power + epsilon)
    scale = jnp.concatenate([scale, pltpu.roll(scale, LANES - group_total, 1)], axis=0)
    member = lax.broadcasted_iota(jnp.int32, (LANES, images), 0) == groups[...]
    member = member.astype(f32)
    picked = lax.dot_general(
        scale, member, (((1,), (0,)), ((), ())), precision=lax.Precision.HIGHEST, preferred_element_type=f32
    )
    logits = sharpness[...] * scores * picked
    logits = jnp.exp(logits - jnp.max(logits, axis=0, keepdims=True))
    result = logits / jnp.sum(logits, axis=0, keepdims=True)
    posteriors[...] = result
    rounded = result.astype(bf16)
    totals = [dot(rounded, weighted[r], ((1,), (0,))) for r in range(rows)]
    for h in range(cols // LANES):
        parts = [total[:, h * LANES : (h + 1) * LANES] for total in totals]
        parts = swap_blocks(parts, LANES // rows)
        for j in range(rows):
            out[h * rows + j] = parts[j].astype(bf16)


def project_body(rows, height, first_row, centre, tilt, received, arrived, out):
    bands, planes, _ = out.shape
    bins = centre.shape[0]
    pairs = arrived.shape[0] * arrived.shape[1]
    by_bin = dot(arrived[...].reshape(pairs, LANES), received[...].reshape(pairs, LANES), ((0,), (0,)))
    width = LANES // rows
    lane = lax.broadcasted_iota(jnp.int32, (bins, LANES), 1)
    empty = jnp.zeros((LANES - bins, 2 * LANES), bf16)
    parts = []
    for r in range(rows):
        deep = centre[...] + tilt[...] * reach_of(first_row[0] + r, planes, height)
        weights = []
        for h in range(2):
            where = ((lane % bands) * planes + h * (planes // 2) + lane // bands).astype(f32)
            weights.append(jnp.maximum(0.0, 1.0 - jnp.abs(where - deep)).astype(bf16))
        weight = jnp.concatenate([empty, jnp.concatenate(weights, axis=1)], axis=0)
        parts.append(dot(by_bin[r * width : (r + 1) * width].astype(bf16), weight, ((1,), (0,))))
    first = swap_blocks([part[:, :LANES] for part in parts], 1)
    second = swap_blocks([part[:, LANES:] for part in parts], 1)
    for j in range(bands):
        out[j] = jnp.concatenate([first[j], second[j]], axis=0).astype(bf16)


def final_body(arrived, out):
    bands = arrived.shape[0]
    wide = arrived[...].astype(f32)
    for zh in range(2):
        for vh in range(bands // 8):
            parts = [wide[vh * 8 + k, zh * 8 : (zh + 1) * 8, :] for k in range(8)]
            parts = swap_blocks(parts, LANES // 8)
            for zl in range(8):
                out[zh * 8 + zl, :, vh * LANES : (vh + 1) * LANES] = parts[zl]


def per_device(volume, images, bin_lists, bin_planes, bin_tilts, defocus, groups, precision):
    bands = lax.axis_size("vol")
    blocks = lax.axis_size("img")
    planes, strip, cols = volume.shape
    image_count, rows, _ = images.shape
    height = rows * bands
    bins = bin_planes.shape[0]
    listed = bin_lists.shape[1]
    group_total = defocus.shape[0]
    first_row = row_of(rows).reshape(1)

    sent = call(
        part_body,
        pltpu.HBM((blocks, planes, LANES), bf16),
        [SMEM, VMEM],
        VMEM,
    )(*in_hbm(bin_lists[0], volume))
    received = lax.all_to_all(sent, "img", 0, 0, tiled=True)

    block = 256
    weighted, square, centre, tilt = call(
        functools.partial(weigh_body, block),
        (
            pltpu.HBM((rows, image_count, cols), bf16),
            jax.ShapeDtypeStruct((rows, 2, group_total, cols), bf16),
            jax.ShapeDtypeStruct((bins, LANES), f32),
            jax.ShapeDtypeStruct((bins, LANES), f32),
        ),
        [SMEM] * 5 + [pl.BlockSpec((block, rows, cols), lambda i: (i, 0, 0))],
        (
            pl.BlockSpec((rows, block, cols), lambda i: (0, i, 0)),
            pl.BlockSpec((rows, 2, group_total, cols), lambda i: (0, 0, 0, 0)),
            pl.BlockSpec((bins, LANES), lambda i: (0, 0)),
            pl.BlockSpec((bins, LANES), lambda i: (0, 0)),
        ),
        scratch=(
            pltpu.VMEM((group_total, rows, cols), f32),
            pltpu.VMEM((rows * rows, rows * rows), bf16),
            pltpu.VMEM((rows, rows, cols), bf16),
            pltpu.VMEM((2, group_total, rows, cols), bf16),
        ),
        grid=(image_count // block,),
        flops=40 * image_count * rows * cols,
        nbytes=4 * image_count * rows * cols,
    )(first_row, *in_hbm(defocus, groups, bin_planes, bin_tilts, images))

    joined = call(
        band_body,
        jax.ShapeDtypeStruct((bands, planes, LANES), bf16),
        [VMEM, VMEM],
        VMEM,
    )(received, centre)
    stack = lax.all_to_all(joined, "vol", 0, 0, tiled=True)
    pieces = call(
        functools.partial(template_body, rows, height),
        jax.ShapeDtypeStruct((blocks, listed, LANES), bf16),
        [SMEM, VMEM, VMEM, VMEM, VMEM],
        VMEM,
    )(first_row, centre, tilt, received, stack)
    templates = lax.all_to_all(pieces, "img", 0, 0, tiled=True)

    payload_rows = listed * (image_count // LANES + 1)
    partial = call(
        score_body,
        jax.ShapeDtypeStruct((bands, payload_rows, LANES), jnp.int16),
        [VMEM, VMEM, VMEM],
        VMEM,
        scratch=(pltpu.VMEM((listed, LANES), f32),),
    )(templates, weighted, square)
    partial = lax.all_to_all(partial, "vol", 0, 0, tiled=True)

    posteriors, spread = call(
        functools.partial(posterior_body, group_total),
        (
            jax.ShapeDtypeStruct((listed, image_count), f32),
            jax.ShapeDtypeStruct((blocks, listed, LANES), bf16),
        ),
        [VMEM, VMEM, VMEM, VMEM],
        (VMEM, VMEM),
    )(partial, groups.reshape(1, image_count), precision.reshape(1, image_count), weighted)
    arrived = lax.all_to_all(spread, "img", 0, 0, tiled=True)

    projected = call(
        functools.partial(project_body, rows, height),
        jax.ShapeDtypeStruct((bands, planes, LANES), bf16),
        [SMEM, VMEM, VMEM, VMEM, VMEM],
        VMEM,
    )(first_row, centre, tilt, received, arrived)
    slabs = lax.all_to_all(projected, "vol", 0, 0, tiled=True)
    numerator = call(
        final_body,
        jax.ShapeDtypeStruct((planes, cols // blocks, height), f32),
        [VMEM],
        VMEM,
    )(slabs)
    return (posteriors.T, numerator.transpose(0, 2, 1))


def solution(mesh):
    placed = (
        P("vol", "img", None),
        P("img", "vol", None),
        P("img", None),
        P(),
        P(),
        P(),
        P("img"),
        P("img"),
    )
    return jax.shard_map(
        per_device,
        mesh=mesh,
        in_specs=placed,
        out_specs=(P("img", None), P("vol", None, "img")),
        check_vma=False,
    )
```

time: 134 us -> 108 us (0.81)
  starting transfers between devices: 49.2 us -> 14.4 us
  blocking collectives: 37.6 us -> 71.1 us
  waiting for transfers between devices: 17.9 us -> 5.91 us
  Pallas kernels: 19.2 us -> 13 us
  local copies, waits for them, and re-layouts: 6.58 us -> 2.2 us
  other arithmetic: 2.09 us -> 0 us
    all_to_all x0 -> x3, blocking collectives: none -> 46.8 us  [the longest x1 16.4 us: per_device(): templates = lax.all_to_all(pieces, 'img', 0, 0, tiled=True)]
    all_to_all x3 -> x1, starting transfers between devices: 33 us -> 14.4 us  [per_device(): received = lax.all_to_all(sent, 'img', 0, 0, tiled=True)]
    ppermute x2 -> x0, starting transfers between devices: 16.2 us -> none  [the longest x1 11.5 us: per_device(): lax.ppermute(bin_lists, 'img', [(i, (i + half_group) % blocks) for i in r...]
    all_to_all x1, blocking collectives: 27.5 us -> 12.8 us  [per_device(): partial = lax.all_to_all(partial, 'vol', 0, 0, tiled=True)]
    all_to_all x3 -> x1, waiting for transfers between devices: 17.3 us -> 5.91 us  [per_device(): received = lax.all_to_all(sent, 'img', 0, 0, tiled=True)]
    pallas_call x5 -> x6, Pallas kernels: 16.5 us -> 10.7 us  [the longest x1 5.43 us: per_device(): call(functools.partial(weigh_body, block), (pltpu.HBM((rows, image_count,...]
    unnamed x18 -> x8, local copies, waits for them, and re-layouts: 5.5 us -> 2.2 us
    all_to_all x1, blocking collectives: 10.1 us -> 11.6 us  [per_device(): slabs = lax.all_to_all(projected, 'vol', 0, 0, tiled=True)]
  transfers between devices with their start and end apart: 5 -> 1, of which waited for: 3 -> 1; matrix products, arithmetic and copies ran while one was open for 2% -> 0% of each run, Pallas kernels for 9% -> 5%
where the time goes in v2:
time: 108 us; the launch traced here: 107 us
  blocking collectives  71.1 us (66%)
  starting transfers between devices  14.4 us (13%)
  Pallas kernels  13 us (12%)
  waiting for transfers between devices  5.91 us (5%)
  local copies, waits for them, and re-layouts  2.2 us (2%)
    all_to_all x1, blocking collectives, per_device(): templates = lax.all_to_all(pieces, 'img', 0, 0, tiled=True)  16.4 us
    all_to_all x1, blocking collectives, per_device(): arrived = lax.all_to_all(spread, 'img', 0, 0, tiled=True)  15.9 us
    all_to_all x1, starting transfers between devices, per_device(): received = lax.all_to_all(sent, 'img', 0, 0, tiled=True)  14.4 us
    all_to_all x1, blocking collectives, per_device(): stack = lax.all_to_all(joined, 'vol', 0, 0, tiled=True)  14.4 us
    all_to_all x1, blocking collectives, per_device(): partial = lax.all_to_all(partial, 'vol', 0, 0, tiled=True)  12.8 us
    all_to_all x1, blocking collectives, per_device(): slabs = lax.all_to_all(projected, 'vol', 0, 0, tiled=True)  11.6 us
    all_to_all x1, waiting for transfers between devices, per_device(): received = lax.all_to_all(sent, 'img', 0, 0, tiled=True)  5.91 us
    pallas_call x1, Pallas kernels, per_device(): call(functools.partial(weigh_body, block), (pltpu.HBM((rows, image_count,...  5.43 us
  transfers between devices with their start and end apart: 1, of which 1 were waited for; matrix products, arithmetic and copies ran while one was open for 0% of the time, Pallas kernels for 5%

profile of v2, /device:TPU:1, one launch (start us, length us, event | category | flops | bytes accessed | tf_op | source)
XLA Modules:
  0.0 107.3 jit_solution(16901682016807846754)
XLA Ops:
  0.6 2.0 %shard_map.96 = bf16[32,16,128]{2,1,0:T(8,128)(2,1)} custom-call(s32[16]{0:T(128)} %bitcast.9, bf16[16,8,256]{2,1,0:T(8,128)(2,1)} %volume.1), custom_call_target="tpu_custom_call" | custom-call | tf_op jit(solution)/shard_map/pallas_call | solution.py:345
  2.6 14.4 %all-to-all-start = ((bf16[32,16,128]{2,1,0:T(8,128)(2,1)}), bf16[32,16,128]{2,1,0:T(8,128)(2,1)S(1)}, u32[]{:S(2)}, u32[]{:S(2)}) async-start(bf16[32,16,128]{2,1,0:T(8,128)(2,1)} %shard_map.96), calls=%async_computation | async-start | bytes 262144 | tf_op jit(solution)/shard_map/all_to_all | solution.py:351
  17.0 5.4 %shard_map.95 = (bf16[16,512,256]{2,1,0:T(8,128)(2,1)}, bf16[16,2,32,256]{3,2,1,0:T(8,128)(2,1)S(1)}, f32[64,128]{1,0:T(8,128)S(1)}, f32[64,128]{1,0:T(8,128)S(1)}) custom-call(s32[1]{0:T(128)} %bitcast.first_row, f32[32]{0:T(128)} %defocus.1, s32[512]{0:T(512)} %groups.1, s32[64]{0:T(128)} %bin_planes.1, f32[64]{0:T(128)} %bin_tilts.1, ...), custom_call_target="tpu_custom_call" | custom-call | flops 83886080 | bytes 8388608 | tf_op jit(solution)/shard_map/pallas_call | solution.py:354
  22.5 0.0 copy-start.2
  22.5 0.0 copy-start.3
  22.5 5.9 %all-to-all-done.received = bf16[32,16,128]{2,1,0:T(8,128)(2,1)S(1)} async-done(((bf16[32,16,128]{2,1,0:T(8,128)(2,1)}), bf16[32,16,128]{2,1,0:T(8,128)(2,1)S(1)}, u32[]{:S(2)}, u32[]{:S(2)}) %all-to-all-start) | async-done | bytes 131104 | tf_op jit(solution)/shard_map/all_to_all | solution.py:351
  28.4 0.1 shard_map.97
  28.5 14.4 %all_to_all.30.planes = bf16[16,16,128]{2,1,0:T(8,128)(2,1)S(1)} all-to-all(bf16[16,16,128]{2,1,0:T(8,128)(2,1)S(1)} %shard_map.97), channel_id=1, replica_groups=mesh['vol'=16,'img'=32] {'vol'}, dimensions={0} | all-to-all | bytes 131072 | tf_op jit(solution)/shard_map/all_to_all | solution.py:386
  42.9 0.5 shard_map.98
  43.4 16.4 %all_to_all.31.templates = bf16[32,16,128]{2,1,0:T(8,128)(2,1)S(1)} all-to-all(bf16[32,16,128]{2,1,0:T(8,128)(2,1)S(1)} %shard_map.98), channel_id=1, replica_groups=mesh['vol'=16,'img'=32] {'img'}, dimensions={0} | all-to-all | bytes 262144 | tf_op jit(solution)/shard_map/all_to_all | solution.py:393
  59.8 0.0 copy-start
  59.8 2.2 %copy-done = bf16[16,512,256]{2,1,0:T(8,128)(2,1)S(1)} copy-done((bf16[16,512,256]{2,1,0:T(8,128)(2,1)S(1)}, bf16[16,512,256]{2,1,0:T(8,128)(2,1)}, u32[]{:S(2)}) %copy-start) | copy-done | bytes 4194328
  62.0 0.0 copy-start.1
  62.0 1.9 %shard_map.99 = s16[16,80,128]{2,1,0:T(8,128)(2,1)S(1)} custom-call(bf16[32,16,128]{2,1,0:T(8,128)(2,1)S(1)} %all_to_all.31.templates, bf16[16,512,256]{2,1,0:T(8,128)(2,1)S(1)} %copy-done, bf16[16,2,32,256]{3,2,1,0:T(8,128)(2,1)S(1)} %get-tuple-element.11.square), custom_call_target="tpu_custom_call" | custom-call | tf_op jit(solution)/shard_map/pallas_call | solution.py:396
  64.0 12.8 %all_to_all.32.partial = s16[16,80,128]{2,1,0:T(8,128)(2,1)S(1)} all-to-all(s16[16,80,128]{2,1,0:T(8,128)(2,1)S(1)} %shard_map.99), channel_id=1, replica_groups=mesh['vol'=16,'img'=32] {'vol'}, dimensions={0} | all-to-all | bytes 655360 | tf_op jit(solution)/shard_map/all_to_all | solution.py:403
  76.7 0.0 copy-done.2
  76.8 0.0 copy-done.3
  76.8 0.0 copy-done.1
  76.8 1.5 %shard_map.100 = (f32[16,512]{1,0:T(8,128)}, bf16[32,16,128]{2,1,0:T(8,128)(2,1)S(1)}) custom-call(s16[16,80,128]{2,1,0:T(8,128)(2,1)S(1)} %all_to_all.32.partial, s32[1,512]{1,0:T(1,128)S(1)} %bitcast.6, f32[1,512]{1,0:T(1,128)S(1)} %bitcast.7, bf16[16,512,256]{2,1,0:T(8,128)(2,1)S(1)} %copy-done.1), custom_call_target="tpu_custom_call" | custom-call | tf_op jit(solution)/shard_map/pallas_call | solution.py:405
  78.2 15.9 %all_to_all.33.arrived = bf16[32,16,128]{2,1,0:T(8,128)(2,1)S(1)} all-to-all(bf16[32,16,128]{2,1,0:T(8,128)(2,1)S(1)} %get-tuple-element.13), channel_id=1, replica_groups=mesh['vol'=16,'img'=32] {'img'}, dimensions={0} | all-to-all | bytes 262144 | tf_op jit(solution)/shard_map/all_to_all | solution.py:414
  94.1 0.7 shard_map.101
  94.9 11.6 %all_to_all.34.arrived = bf16[16,16,128]{2,1,0:T(8,128)(2,1)S(1)} all-to-all(bf16[16,16,128]{2,1,0:T(8,128)(2,1)S(1)} %shard_map.101), channel_id=1, replica_groups=mesh['vol'=16,'img'=32] {'vol'}, dimensions={0} | all-to-all | bytes 131072 | tf_op jit(solution)/shard_map/all_to_all | solution.py:422
  106.4 0.9 shard_map.102
Async XLA Ops:
  2.6 25.8 %all-to-all-start = ((bf16[32,16,128]{2,1,0:T(8,128)(2,1)}), bf16[32,16,128]{2,1,0:T(8,128)(2,1)S(1)}, u32[]{:S(2)}, u32[]{:S(2)}) async-start(bf16[32,16,128]{2,1,0:T(8,128)(2,1)} %shard_map.96), calls=%async_computation | async-start | bytes 262144 | tf_op jit(solution)/shard_map/all_to_all | solution.py:351
  22.5 54.3 %copy-start.2 = (s32[512]{0:T(512)S(1)}, s32[512]{0:T(512)}, u32[]{:S(2)}) copy-start(s32[512]{0:T(512)} %groups.1) | copy-start | bytes 6148
  22.5 54.3 %copy-start.3 = (f32[512]{0:T(512)S(1)}, f32[512]{0:T(512)}, u32[]{:S(2)}) copy-start(f32[512]{0:T(512)} %param.15) | copy-start | bytes 6148
  59.8 2.2 %copy-start = (bf16[16,512,256]{2,1,0:T(8,128)(2,1)S(1)}, bf16[16,512,256]{2,1,0:T(8,128)(2,1)}, u32[]{:S(2)}) copy-start(bf16[16,512,256]{2,1,0:T(8,128)(2,1)} %get-tuple-element.10.weighted) | copy-start | bytes 12582916
  62.0 14.7 %copy-start.1 = (bf16[16,512,256]{2,1,0:T(8,128)(2,1)S(1)}, bf16[16,512,256]{2,1,0:T(8,128)(2,1)}, u32[]{:S(2)}) copy-start(bf16[16,512,256]{2,1,0:T(8,128)(2,1)} %get-tuple-element.10.weighted) | copy-start | bytes 12582916

commit v3 on v2

--- a/solution.py
+++ b/solution.py
@@ -89,23 +89,21 @@
     there = lax.broadcasted_iota(jnp.int32, (size, size), 1)
     mixer = one_hot((here % planes) * strip + here // planes == there)
     mixed = dot(mixer, volume[...].astype(f32).reshape(size, cols).astype(bf16), ((1,), (0,)))
-    place = lax.broadcasted_iota(jnp.int32, (planes, LANES), 0)
     lane = lax.broadcasted_iota(jnp.int32, (planes, LANES), 1)
     half = LANES // 2
-    hit = (place == 0) & (lane == lists[0] + half)
-    for o in range(1, planes):
-        hit = hit | ((place == o) & (lane == lists[o] + half))
-    listed = hit.astype(f32)
-    for h in range(cols // LANES):
-        parts = [mixed[r * planes : (r + 1) * planes, h * LANES : (h + 1) * LANES] for r in range(strip)]
-        parts = swap_blocks(parts, half // strip)
-        for j in range(strip):
-            piece = parts[j]
-            out[h * 2 * strip + j] = jnp.where(lane < half, piece, listed).astype(bf16)
-            out[h * 2 * strip + strip + j] = jnp.where(lane < half, pltpu.roll(piece, half, 1), listed).astype(bf16)
-
-
-def weigh_body(block, first_row, defocus, groups, bin_planes, bin_tilts, images, out, square, centre, tilt, table, mixer, held, power):
+    ids = jnp.concatenate([lists[...], jnp.zeros((1, LANES - planes), jnp.int32)], axis=1)
+    ids = jnp.sum(jnp.where(diagonal(planes), ids, 0), axis=1, keepdims=True)
+    listed = (lane == ids + half).astype(f32)
+    place = 0
+    for r in range(strip):
+        for h in range(cols // LANES):
+            piece = mixed[r * planes : (r + 1) * planes, h * LANES : (h + 1) * LANES]
+            out[place] = jnp.where(lane < half, piece, listed).astype(bf16)
+            out[place + 1] = jnp.where(lane < half, pltpu.roll(piece, half, 1), listed).astype(bf16)
+            place += 2
+
+
+def weigh_body(block, first_row, defocus, groups, bin_planes, bin_tilts, received, images, out, square, chosen, centre, tilt, table, mixer, held, power):
     _, rows, cols = images.shape
     group_total = table.shape[0]
 
@@ -135,6 +133,7 @@
             for g in range(0, group_total, rows):
                 mixed = dot(mixer[...], power[part, g : g + rows].reshape(rows * rows, cols), ((1,), (0,)))
                 square[:, part, g : g + rows, :] = mixed.astype(bf16).reshape(rows, rows, cols)
+        chosen[...] = received[...]
         for q in range(centre.shape[0]):
             centre[q : q + 1, :] = jnp.full((1, LANES), bin_planes[q].astype(f32))
             tilt[q : q + 1, :] = jnp.full((1, LANES), bin_tilts[q])
@@ -152,30 +151,20 @@
     lax.fori_loop(0, block // rows, some, 0, unroll=True)
 
 
-def band_body(received, after, out):
-    lane = lax.broadcasted_iota(jnp.int32, received.shape[1:], 1)
-    half = LANES // 2
-    for w in range(out.shape[0]):
-        first = received[2 * w].astype(f32)
-        second = pltpu.roll(received[2 * w + 1].astype(f32), half, 1)
-        out[w] = jnp.where(lane < half, first, second).astype(bf16)
-
-
-def template_body(rows, height, first_row, centre, tilt, received, planes, out):
-    bands, slab, _ = planes.shape
+def template_body(strip, height, row, centre, tilt, received, planes, out):
+    bands = planes.shape[0]
+    slab = planes.shape[1] // 2
     bins = centre.shape[0]
     total = bands * slab
     where = lax.broadcasted_iota(jnp.int32, (bins, total), 1).astype(f32)
-    weights = []
-    for r in range(rows):
-        deep = centre[...] + tilt[...] * reach_of(first_row[0] + r, slab, height)
+    tables = []
+    for h in range(2):
+        deep = centre[...] + tilt[...] * reach_of(row[0] + h * strip, slab, height)
         deep = jnp.concatenate([deep] * (total // LANES), axis=1)
-        weights.append(jnp.maximum(0.0, 1.0 - jnp.abs(where - deep)).astype(bf16))
-    every = dot(jnp.concatenate(weights, axis=0), planes[...].reshape(total, LANES), ((1,), (0,)))
+        weight = jnp.maximum(0.0, 1.0 - jnp.abs(where - deep)).astype(bf16)
+        tables.append(dot(weight, planes[:, h * slab : (h + 1) * slab, :].reshape(total, LANES), ((1,), (0,))))
     lane = lax.broadcasted_iota(jnp.int32, (bins, LANES), 1)
-    table = every[:bins]
-    for r in range(1, rows):
-        table = jnp.where(lane // (LANES // rows) == r, every[r * bins : (r + 1) * bins], table)
+    table = jnp.where(lane < LANES // 2, tables[0], pltpu.roll(tables[1], LANES // 2, 1))
     table = jnp.concatenate([jnp.zeros((LANES - bins, LANES), bf16), table.astype(bf16)], axis=0)
     chosen = received[...].reshape(-1, LANES)
     out[...] = dot(chosen, table, ((1,), (0,))).astype(bf16).reshape(out.shape)
@@ -204,12 +193,17 @@
     listed = templates.shape[1]
     total = None
     power = None
-    halves = []
-    for h in range(cols // LANES):
-        parts = [templates[h * rows + j].astype(f32) for j in range(rows)]
-        halves.append(swap_blocks(parts, LANES // rows))
+    lane = lax.broadcasted_iota(jnp.int32, (listed, LANES), 1)
+    pieces = [None] * rows
+    strip = rows // 2
+    half = LANES // 2
+    for r in range(strip):
+        parts = [templates[4 * r + k].astype(f32) for k in range(4)]
+        turned = [pltpu.roll(part, half, 1) for part in parts]
+        pieces[r] = [jnp.where(lane < half, parts[k], turned[k + 1]) for k in (0, 2)]
+        pieces[strip + r] = [jnp.where(lane < half, turned[k], parts[k + 1]) for k in (0, 2)]
     for r in range(rows):
-        piece = jnp.concatenate([half[r] for half in halves], axis=1).astype(bf16)
+        piece = jnp.concatenate(pieces[r], axis=1).astype(bf16)
         part = dot(piece, weighted[r], ((1,), (1,)))
         total = part if total is None else total + part
         wide = piece.astype(f32)
@@ -344,25 +338,32 @@
 
     sent = call(
         part_body,
-        pltpu.HBM((blocks, planes, LANES), bf16),
-        [SMEM, VMEM],
+        pltpu.VMEM((blocks, planes, LANES), bf16),
+        [VMEM, VMEM],
         VMEM,
-    )(*in_hbm(bin_lists[0], volume))
+    )(*in_hbm(bin_lists, volume))
     received = lax.all_to_all(sent, "img", 0, 0, tiled=True)
+    stack = lax.all_to_all(received.reshape(bands, 2 * planes, LANES), "vol", 0, 0, tiled=True)
 
     block = 256
-    weighted, square, centre, tilt = call(
+    weighted, square, chosen, centre, tilt = call(
         functools.partial(weigh_body, block),
         (
             pltpu.HBM((rows, image_count, cols), bf16),
             jax.ShapeDtypeStruct((rows, 2, group_total, cols), bf16),
+            jax.ShapeDtypeStruct((blocks, planes, LANES), bf16),
             jax.ShapeDtypeStruct((bins, LANES), f32),
             jax.ShapeDtypeStruct((bins, LANES), f32),
         ),
-        [SMEM] * 5 + [pl.BlockSpec((block, rows, cols), lambda i: (i, 0, 0))],
+        [SMEM] * 5
+        + [
+            pl.BlockSpec((blocks, planes, LANES), lambda i: (0, 0, 0)),
+            pl.BlockSpec((block, rows, cols), lambda i: (i, 0, 0)),
+        ],
         (
             pl.BlockSpec((rows, block, cols), lambda i: (0, i, 0)),
             pl.BlockSpec((rows, 2, group_total, cols), lambda i: (0, 0, 0, 0)),
+            pl.BlockSpec((blocks, planes, LANES), lambda i: (0, 0, 0)),
             pl.BlockSpec((bins, LANES), lambda i: (0, 0)),
             pl.BlockSpec((bins, LANES), lambda i: (0, 0)),
         ),
@@ -375,21 +376,16 @@
         grid=(image_count // block,),
         flops=40 * image_count * rows * cols,
         nbytes=4 * image_count * rows * cols,
-    )(first_row, *in_hbm(defocus, groups, bin_planes, bin_tilts, images))
-
-    joined = call(
-        band_body,
-        jax.ShapeDtypeStruct((bands, planes, LANES), bf16),
-        [VMEM, VMEM],
-        VMEM,
-    )(received, centre)
-    stack = lax.all_to_all(joined, "vol", 0, 0, tiled=True)
+    )(first_row, *in_hbm(defocus, groups, bin_planes, bin_tilts, received, images))
+
     pieces = call(
-        functools.partial(template_body, rows, height),
+        functools.partial(template_body, strip, height),
         jax.ShapeDtypeStruct((blocks, listed, LANES), bf16),
         [SMEM, VMEM, VMEM, VMEM, VMEM],
         VMEM,
-    )(first_row, centre, tilt, received, stack)
+        flops=2**33,
+        nbytes=2**25,
+    )(first_row + lax.axis_index("img") // 4, centre, tilt, chosen, stack)
     templates = lax.all_to_all(pieces, "img", 0, 0, tiled=True)
 
     payload_rows = listed * (image_count // LANES + 1)
@@ -418,7 +414,7 @@
         jax.ShapeDtypeStruct((bands, planes, LANES), bf16),
         [SMEM, VMEM, VMEM, VMEM, VMEM],
         VMEM,
-    )(first_row, centre, tilt, received, arrived)
+    )(first_row, centre, tilt, chosen, arrived)
     slabs = lax.all_to_all(projected, "vol", 0, 0, tiled=True)
     numerator = call(
         final_body,

time: 108 us -> 105 us (0.972)
  blocking collectives: 71.1 us -> 83.2 us
  starting transfers between devices: 14.4 us -> 7.24 us
  waiting for transfers between devices: 5.91 us -> 1.93 us
  local copies, waits for them, and re-layouts: 2.2 us -> 0.02 us
  Pallas kernels: 13 us -> 11.7 us
    all_to_all x1, blocking collectives: 14.4 us -> 25.7 us  [per_device(): received = lax.all_to_all(sent, 'img', 0, 0, tiled=True)]
    all_to_all x1, starting transfers between devices: 14.4 us -> 7.24 us  [per_device(): lax.all_to_all(received.reshape(bands, 2 * planes, LANES), 'vol', 0, 0, t...]
    all_to_all x1, waiting for transfers between devices: 5.91 us -> 1.93 us  [per_device(): lax.all_to_all(received.reshape(bands, 2 * planes, LANES), 'vol', 0, 0, t...]
    unnamed x8 -> x6, local copies, waits for them, and re-layouts: 2.2 us -> 0.02 us
    all_to_all x1, blocking collectives: 12.8 us -> 14.3 us  [per_device(): partial = lax.all_to_all(partial, 'vol', 0, 0, tiled=True)]
    pallas_call x3 -> x2, Pallas kernels: 2.56 us -> 1.46 us  [the longest x1 1.08 us: per_device(): call(part_body, pltpu.VMEM((blocks, planes, LANES), bf16), [VMEM, VMEM],...]
where the time goes in v3:
time: 105 us
  blocking collectives  83.2 us (79%)
  Pallas kernels  11.7 us (11%)
  starting transfers between devices  7.24 us (7%)
  waiting for transfers between devices  1.93 us (2%)
    all_to_all x1, blocking collectives, per_device(): received = lax.all_to_all(sent, 'img', 0, 0, tiled=True)  25.7 us
    all_to_all x1, blocking collectives, per_device(): templates = lax.all_to_all(pieces, 'img', 0, 0, tiled=True)  15.9 us
    all_to_all x1, blocking collectives, per_device(): arrived = lax.all_to_all(spread, 'img', 0, 0, tiled=True)  15.8 us
    all_to_all x1, blocking collectives, per_device(): partial = lax.all_to_all(partial, 'vol', 0, 0, tiled=True)  14.3 us
    all_to_all x1, blocking collectives, per_device(): slabs = lax.all_to_all(projected, 'vol', 0, 0, tiled=True)  11.6 us
    all_to_all x1, starting transfers between devices, per_device(): lax.all_to_all(received.reshape(bands, 2 * planes, LANES), 'vol', 0, 0, t...  7.24 us
    pallas_call x1, Pallas kernels, per_device(): call(functools.partial(weigh_body, block), (pltpu.HBM((rows, image_count,...  5.48 us
  transfers between devices with their start and end apart: 1, of which 1 were waited for; matrix products, arithmetic and copies ran while one was open for 0% of the time, Pallas kernels for 5%

profile of v3, /device:TPU:1, one launch (start us, length us, event | category | flops | bytes accessed | tf_op | source)
XLA Modules:
  0.0 104.8 jit_solution(10601009782772048129)
XLA Ops:
  0.6 1.1 %shard_map.95 = bf16[32,16,128]{2,1,0:T(8,128)(2,1)S(1)} custom-call(s32[1,16]{1,0:T(1,128)} %lists.1, bf16[16,8,256]{2,1,0:T(8,128)(2,1)} %volume.1), custom_call_target="tpu_custom_call" | custom-call | tf_op jit(solution)/shard_map/pallas_call | solution.py:339
  1.7 25.7 %all_to_all.30.received = bf16[32,16,128]{2,1,0:T(8,128)(2,1)} all-to-all(bf16[32,16,128]{2,1,0:T(8,128)(2,1)S(1)} %shard_map.95), channel_id=1, replica_groups=mesh['vol'=16,'img'=32] {'img'}, dimensions={0} | all-to-all | bytes 262144 | tf_op jit(solution)/shard_map/all_to_all | solution.py:345
  27.4 7.2 %all-to-all-start.1 = ((bf16[16,32,128]{2,1,0:T(8,128)(2,1)}), bf16[16,32,128]{2,1,0:T(8,128)(2,1)S(1)}, u32[]{:S(2)}, u32[]{:S(2)}) async-start(bf16[16,32,128]{2,1,0:T(8,128)(2,1)} %bitcast.2), calls=%async_computation.1 | async-start | bytes 262144 | tf_op jit(solution)/shard_map/all_to_all | solution.py:346
  34.7 5.5 %shard_map.96 = (bf16[16,512,256]{2,1,0:T(8,128)(2,1)}, bf16[16,2,32,256]{3,2,1,0:T(8,128)(2,1)S(1)}, bf16[32,16,128]{2,1,0:T(8,128)(2,1)S(1)}, f32[64,128]{1,0:T(8,128)S(1)}, f32[64,128]{1,0:T(8,128)S(1)}) custom-call(s32[1]{0:T(128)} %bitcast.first_row, f32[32]{0:T(128)} %defocus.1, s32[512]{0:T(512)} %groups.1, s32[64]{0:T(128)} %bin_planes.1, ...), custom_call_target="tpu_custom_call" | custom-call | flops 83886080 | bytes 8388608 | tf_op jit(solution)/shard_map/pallas_call | solution.py:349
  40.1 1.9 %all-to-all-done.1.planes = bf16[16,32,128]{2,1,0:T(8,128)(2,1)S(1)} async-done(((bf16[16,32,128]{2,1,0:T(8,128)(2,1)}), bf16[16,32,128]{2,1,0:T(8,128)(2,1)S(1)}, u32[]{:S(2)}, u32[]{:S(2)}) %all-to-all-start.1) | async-done | bytes 131104 | tf_op jit(solution)/shard_map/all_to_all | solution.py:346
  42.1 0.0 copy-start
  42.1 0.4 shard_map.97
  42.5 0.0 copy-start.1
  42.5 0.0 copy-start.2
  42.5 15.9 %all_to_all.31.templates = bf16[32,16,128]{2,1,0:T(8,128)(2,1)S(1)} all-to-all(bf16[32,16,128]{2,1,0:T(8,128)(2,1)S(1)} %shard_map.97), channel_id=1, replica_groups=mesh['vol'=16,'img'=32] {'img'}, dimensions={0} | all-to-all | bytes 262144 | tf_op jit(solution)/shard_map/all_to_all | solution.py:389
  58.3 0.0 copy-done
  58.3 1.6 %shard_map.98 = s16[16,80,128]{2,1,0:T(8,128)(2,1)S(1)} custom-call(bf16[32,16,128]{2,1,0:T(8,128)(2,1)S(1)} %all_to_all.31.templates, bf16[16,512,256]{2,1,0:T(8,128)(2,1)S(1)} %copy-done, bf16[16,2,32,256]{3,2,1,0:T(8,128)(2,1)S(1)} %get-tuple-element.13.square), custom_call_target="tpu_custom_call" | custom-call | tf_op jit(solution)/shard_map/pallas_call | solution.py:392
  60.0 14.3 %all_to_all.32.partial = s16[16,80,128]{2,1,0:T(8,128)(2,1)S(1)} all-to-all(s16[16,80,128]{2,1,0:T(8,128)(2,1)S(1)} %shard_map.98), channel_id=1, replica_groups=mesh['vol'=16,'img'=32] {'vol'}, dimensions={0} | all-to-all | bytes 655360 | tf_op jit(solution)/shard_map/all_to_all | solution.py:399
  74.3 0.0 copy-done.1
  74.3 0.0 copy-done.2
  74.3 1.5 %shard_map.99 = (f32[16,512]{1,0:T(8,128)}, bf16[32,16,128]{2,1,0:T(8,128)(2,1)S(1)}) custom-call(s16[16,80,128]{2,1,0:T(8,128)(2,1)S(1)} %all_to_all.32.partial, s32[1,512]{1,0:T(1,128)S(1)} %bitcast.7, f32[1,512]{1,0:T(1,128)S(1)} %bitcast.8, bf16[16,512,256]{2,1,0:T(8,128)(2,1)S(1)} %copy-done), custom_call_target="tpu_custom_call" | custom-call | tf_op jit(solution)/shard_map/pallas_call | solution.py:401
  75.8 15.8 %all_to_all.33.arrived = bf16[32,16,128]{2,1,0:T(8,128)(2,1)S(1)} all-to-all(bf16[32,16,128]{2,1,0:T(8,128)(2,1)S(1)} %get-tuple-element.15), channel_id=1, replica_groups=mesh['vol'=16,'img'=32] {'img'}, dimensions={0} | all-to-all | bytes 262144 | tf_op jit(solution)/shard_map/all_to_all | solution.py:410
  91.5 0.7 shard_map.100
  92.3 11.6 %all_to_all.34.arrived = bf16[16,16,128]{2,1,0:T(8,128)(2,1)S(1)} all-to-all(bf16[16,16,128]{2,1,0:T(8,128)(2,1)S(1)} %shard_map.100), channel_id=1, replica_groups=mesh['vol'=16,'img'=32] {'vol'}, dimensions={0} | all-to-all | bytes 131072 | tf_op jit(solution)/shard_map/all_to_all | solution.py:418
  103.9 0.9 shard_map.101
Async XLA Ops:
  27.4 14.7 %all-to-all-start.1 = ((bf16[16,32,128]{2,1,0:T(8,128)(2,1)}), bf16[16,32,128]{2,1,0:T(8,128)(2,1)S(1)}, u32[]{:S(2)}, u32[]{:S(2)}) async-start(bf16[16,32,128]{2,1,0:T(8,128)(2,1)} %bitcast.2), calls=%async_computation.1 | async-start | bytes 262144 | tf_op jit(solution)/shard_map/all_to_all | solution.py:346
  42.1 16.3 %copy-start = (bf16[16,512,256]{2,1,0:T(8,128)(2,1)S(1)}, bf16[16,512,256]{2,1,0:T(8,128)(2,1)}, u32[]{:S(2)}) copy-start(bf16[16,512,256]{2,1,0:T(8,128)(2,1)} %get-tuple-element.12.weighted) | copy-start | bytes 12582916
  42.5 31.8 %copy-start.1 = (s32[512]{0:T(512)S(1)}, s32[512]{0:T(512)}, u32[]{:S(2)}) copy-start(s32[512]{0:T(512)} %groups.1) | copy-start | bytes 6148
  42.5 31.8 %copy-start.2 = (f32[512]{0:T(512)S(1)}, f32[512]{0:T(512)}, u32[]{:S(2)}) copy-start(f32[512]{0:T(512)} %param.15) | copy-start | bytes 6148

commit v4 on v3

--- a/solution.py
+++ b/solution.py
@@ -174,8 +174,7 @@
 
 
 def level_code(largest):
-    code = jnp.floor(256.0 * jnp.log2(jnp.maximum(largest, 1e-30))) + 2.0
-    return code, jnp.exp2(code * (-1.0 / 256.0))
+    return jnp.floor(256.0 * jnp.log2(jnp.maximum(largest, 1e-30))) + 2.0
 
 
 def level_of(code):
@@ -218,12 +217,11 @@
     extra[...] = jnp.zeros_like(extra)
     extra[:, :group_total] = power
     power = jnp.maximum(extra[...], 0.0)
-    row_code, row_scale = level_code(jnp.max(jnp.abs(total), axis=1, keepdims=True))
-    total = total * row_scale
-    image_code, image_scale = level_code(jnp.max(jnp.abs(total), axis=0, keepdims=True))
-    total = jnp.clip(jnp.floor(total * image_scale * top + 0.5), -top, top)
-    power_code, power_scale = level_code(jnp.max(power, axis=1, keepdims=True))
-    power = jnp.minimum(power * power_scale, 1.0) * top
+    power_code = level_code(jnp.max(power, axis=1, keepdims=True))
+    power = jnp.minimum(power * level_of(-power_code), 1.0) * top
+    total = total * level_of(-0.5 * power_code)
+    image_code = level_code(jnp.max(jnp.abs(total), axis=0, keepdims=True))
+    total = jnp.clip(jnp.floor(total * level_of(-image_code) * top + 0.5), -top, top)
     high = jnp.floor(power)
     low = jnp.floor((power - high) * top + 0.5)
     half = listed // 2
@@ -237,9 +235,9 @@
     for c in range(chunks):
         extra[half + c : half + c + 1, :] = image_code[:, c * LANES : (c + 1) * LANES]
     square_mask = diagonal(listed)
-    for place, code in ((half + chunks, row_code), (half + chunks + 1, power_code)):
-        extra[place : place + 1, :] = jnp.sum(jnp.where(square_mask, code, 0.0), axis=0, keepdims=True)
-    extra[half + chunks + 2 :, :] = jnp.zeros((listed - half - chunks - 2, LANES), f32)
+    place = half + chunks
+    extra[place : place + 1, :] = jnp.sum(jnp.where(square_mask, power_code, 0.0), axis=0, keepdims=True)
+    extra[place + 1 :, :] = jnp.zeros((listed - place - 1, LANES), f32)
     pieces = [total[:, c * LANES : (c + 1) * LANES] for c in range(chunks)] + [extra[...]]
     pieces = [piece.astype(jnp.int32).astype(jnp.int16) for piece in pieces]
     for k in range(out.shape[0]):
@@ -259,10 +257,10 @@
     for k in range(partial.shape[0]):
         value = partial[k].astype(jnp.int32).astype(f32)
         extra = value[chunks * listed :]
-        row_level, power_level = (
-            level_of(jnp.sum(jnp.where(square_mask, extra[place : place + 1], 0.0), axis=1, keepdims=True)) / top
-            for place in (half + chunks, half + chunks + 1)
-        )
+        place = half + chunks
+        power_code = jnp.sum(jnp.where(square_mask, extra[place : place + 1], 0.0), axis=1, keepdims=True)
+        row_level = level_of(0.5 * power_code) * (1.0 / top)
+        power_level = level_of(power_code) * (1.0 / top)
         image_level = [level_of(extra[half + c : half + c + 1]) for c in range(chunks)]
         part = [value[c * listed : (c + 1) * listed] * row_level * image_level[c] for c in range(chunks)]
         scores = part if scores is None else [a + b for a, b in zip(scores, part)]

time: 105 us -> 105 us (level)
  no operation moved by 1% of the time
where the time goes in v4:
time: 105 us
  blocking collectives  83.2 us (79%)
  Pallas kernels  11.7 us (11%)
  starting transfers between devices  7.24 us (7%)
  waiting for transfers between devices  1.93 us (2%)
    all_to_all x1, blocking collectives, per_device(): received = lax.all_to_all(sent, 'img', 0, 0, tiled=True)  25.7 us
    all_to_all x1, blocking collectives, per_device(): templates = lax.all_to_all(pieces, 'img', 0, 0, tiled=True)  15.9 us
    all_to_all x1, blocking collectives, per_device(): arrived = lax.all_to_all(spread, 'img', 0, 0, tiled=True)  15.8 us
    all_to_all x1, blocking collectives, per_device(): partial = lax.all_to_all(partial, 'vol', 0, 0, tiled=True)  14.3 us
    all_to_all x1, blocking collectives, per_device(): slabs = lax.all_to_all(projected, 'vol', 0, 0, tiled=True)  11.6 us
    all_to_all x1, starting transfers between devices, per_device(): lax.all_to_all(received.reshape(bands, 2 * planes, LANES), 'vol', 0, 0, t...  7.24 us
    pallas_call x1, Pallas kernels, per_device(): call(functools.partial(weigh_body, block), (pltpu.HBM((rows, image_count,...  5.48 us
  transfers between devices with their start and end apart: 1, of which 1 were waited for; matrix products, arithmetic and copies ran while one was open for 0% of the time, Pallas kernels for 5%

profile of v4, /device:TPU:1, one launch (start us, length us, event | category | flops | bytes accessed | tf_op | source)
XLA Modules:
  0.0 104.8 jit_solution(16900927270484621609)
XLA Ops:
  0.6 1.1 %shard_map.95 = bf16[32,16,128]{2,1,0:T(8,128)(2,1)S(1)} custom-call(s32[1,16]{1,0:T(1,128)} %lists.1, bf16[16,8,256]{2,1,0:T(8,128)(2,1)} %volume.1), custom_call_target="tpu_custom_call" | custom-call | tf_op jit(solution)/shard_map/pallas_call | solution.py:337
  1.7 25.7 %all_to_all.30.received = bf16[32,16,128]{2,1,0:T(8,128)(2,1)} all-to-all(bf16[32,16,128]{2,1,0:T(8,128)(2,1)S(1)} %shard_map.95), channel_id=1, replica_groups=mesh['vol'=16,'img'=32] {'img'}, dimensions={0} | all-to-all | bytes 262144 | tf_op jit(solution)/shard_map/all_to_all | solution.py:343
  27.4 7.2 %all-to-all-start.1 = ((bf16[16,32,128]{2,1,0:T(8,128)(2,1)}), bf16[16,32,128]{2,1,0:T(8,128)(2,1)S(1)}, u32[]{:S(2)}, u32[]{:S(2)}) async-start(bf16[16,32,128]{2,1,0:T(8,128)(2,1)} %bitcast.2), calls=%async_computation.1 | async-start | bytes 262144 | tf_op jit(solution)/shard_map/all_to_all | solution.py:344
  34.7 5.5 %shard_map.96 = (bf16[16,512,256]{2,1,0:T(8,128)(2,1)}, bf16[16,2,32,256]{3,2,1,0:T(8,128)(2,1)S(1)}, bf16[32,16,128]{2,1,0:T(8,128)(2,1)S(1)}, f32[64,128]{1,0:T(8,128)S(1)}, f32[64,128]{1,0:T(8,128)S(1)}) custom-call(s32[1]{0:T(128)} %bitcast.first_row, f32[32]{0:T(128)} %defocus.1, s32[512]{0:T(512)} %groups.1, s32[64]{0:T(128)} %bin_planes.1, ...), custom_call_target="tpu_custom_call" | custom-call | flops 83886080 | bytes 8388608 | tf_op jit(solution)/shard_map/pallas_call | solution.py:347
  40.1 1.9 %all-to-all-done.1.planes = bf16[16,32,128]{2,1,0:T(8,128)(2,1)S(1)} async-done(((bf16[16,32,128]{2,1,0:T(8,128)(2,1)}), bf16[16,32,128]{2,1,0:T(8,128)(2,1)S(1)}, u32[]{:S(2)}, u32[]{:S(2)}) %all-to-all-start.1) | async-done | bytes 131104 | tf_op jit(solution)/shard_map/all_to_all | solution.py:344
  42.1 0.0 copy-start
  42.1 0.4 shard_map.97
  42.5 0.0 copy-start.1
  42.5 0.0 copy-start.2
  42.5 15.9 %all_to_all.31.templates = bf16[32,16,128]{2,1,0:T(8,128)(2,1)S(1)} all-to-all(bf16[32,16,128]{2,1,0:T(8,128)(2,1)S(1)} %shard_map.97), channel_id=1, replica_groups=mesh['vol'=16,'img'=32] {'img'}, dimensions={0} | all-to-all | bytes 262144 | tf_op jit(solution)/shard_map/all_to_all | solution.py:387
  58.3 0.0 copy-done
  58.3 1.6 %shard_map.98 = s16[16,80,128]{2,1,0:T(8,128)(2,1)S(1)} custom-call(bf16[32,16,128]{2,1,0:T(8,128)(2,1)S(1)} %all_to_all.31.templates, bf16[16,512,256]{2,1,0:T(8,128)(2,1)S(1)} %copy-done, bf16[16,2,32,256]{3,2,1,0:T(8,128)(2,1)S(1)} %get-tuple-element.13.square), custom_call_target="tpu_custom_call" | custom-call | tf_op jit(solution)/shard_map/pallas_call | solution.py:390
  60.0 14.3 %all_to_all.32.partial = s16[16,80,128]{2,1,0:T(8,128)(2,1)S(1)} all-to-all(s16[16,80,128]{2,1,0:T(8,128)(2,1)S(1)} %shard_map.98), channel_id=1, replica_groups=mesh['vol'=16,'img'=32] {'vol'}, dimensions={0} | all-to-all | bytes 655360 | tf_op jit(solution)/shard_map/all_to_all | solution.py:397
  74.3 0.0 copy-done.1
  74.3 0.0 copy-done.2
  74.3 1.5 %shard_map.99 = (f32[16,512]{1,0:T(8,128)}, bf16[32,16,128]{2,1,0:T(8,128)(2,1)S(1)}) custom-call(s16[16,80,128]{2,1,0:T(8,128)(2,1)S(1)} %all_to_all.32.partial, s32[1,512]{1,0:T(1,128)S(1)} %bitcast.7, f32[1,512]{1,0:T(1,128)S(1)} %bitcast.8, bf16[16,512,256]{2,1,0:T(8,128)(2,1)S(1)} %copy-done), custom_call_target="tpu_custom_call" | custom-call | tf_op jit(solution)/shard_map/pallas_call | solution.py:399
  75.8 15.8 %all_to_all.33.arrived = bf16[32,16,128]{2,1,0:T(8,128)(2,1)S(1)} all-to-all(bf16[32,16,128]{2,1,0:T(8,128)(2,1)S(1)} %get-tuple-element.15), channel_id=1, replica_groups=mesh['vol'=16,'img'=32] {'img'}, dimensions={0} | all-to-all | bytes 262144 | tf_op jit(solution)/shard_map/all_to_all | solution.py:408
  91.6 0.7 shard_map.100
  92.3 11.6 %all_to_all.34.arrived = bf16[16,16,128]{2,1,0:T(8,128)(2,1)S(1)} all-to-all(bf16[16,16,128]{2,1,0:T(8,128)(2,1)S(1)} %shard_map.100), channel_id=1, replica_groups=mesh['vol'=16,'img'=32] {'vol'}, dimensions={0} | all-to-all | bytes 131072 | tf_op jit(solution)/shard_map/all_to_all | solution.py:416
  103.9 0.9 shard_map.101
Async XLA Ops:
  27.4 14.7 %all-to-all-start.1 = ((bf16[16,32,128]{2,1,0:T(8,128)(2,1)}), bf16[16,32,128]{2,1,0:T(8,128)(2,1)S(1)}, u32[]{:S(2)}, u32[]{:S(2)}) async-start(bf16[16,32,128]{2,1,0:T(8,128)(2,1)} %bitcast.2), calls=%async_computation.1 | async-start | bytes 262144 | tf_op jit(solution)/shard_map/all_to_all | solution.py:344
  42.1 16.3 %copy-start = (bf16[16,512,256]{2,1,0:T(8,128)(2,1)S(1)}, bf16[16,512,256]{2,1,0:T(8,128)(2,1)}, u32[]{:S(2)}) copy-start(bf16[16,512,256]{2,1,0:T(8,128)(2,1)} %get-tuple-element.12.weighted) | copy-start | bytes 12582916
  42.5 31.8 %copy-start.1 = (s32[512]{0:T(512)S(1)}, s32[512]{0:T(512)}, u32[]{:S(2)}) copy-start(s32[512]{0:T(512)} %groups.1) | copy-start | bytes 6148
  42.5 31.8 %copy-start.2 = (f32[512]{0:T(512)S(1)}, f32[512]{0:T(512)}, u32[]{:S(2)}) copy-start(f32[512]{0:T(512)} %param.15) | copy-start | bytes 6148

commit v5 on v4

--- a/solution.py
+++ b/solution.py
@@ -84,23 +84,26 @@
 
 def part_body(lists, volume, out):
     planes, strip, cols = volume.shape
+    listed = lists.shape[1]
     size = planes * strip
     here = lax.broadcasted_iota(jnp.int32, (size, size), 0)
     there = lax.broadcasted_iota(jnp.int32, (size, size), 1)
     mixer = one_hot((here % planes) * strip + here // planes == there)
     mixed = dot(mixer, volume[...].astype(f32).reshape(size, cols).astype(bf16), ((1,), (0,)))
-    lane = lax.broadcasted_iota(jnp.int32, (planes, LANES), 1)
+    ids = jnp.concatenate([lists[...], jnp.zeros((1, LANES - listed), jnp.int32)], axis=1)
+    ids = jnp.sum(jnp.where(diagonal(listed), ids, 0), axis=1, keepdims=True)
+    lane = lax.broadcasted_iota(jnp.int32, (listed // 2, LANES), 1)
     half = LANES // 2
-    ids = jnp.concatenate([lists[...], jnp.zeros((1, LANES - planes), jnp.int32)], axis=1)
-    ids = jnp.sum(jnp.where(diagonal(planes), ids, 0), axis=1, keepdims=True)
-    listed = (lane == ids + half).astype(f32)
+    hit = lane == jnp.where(lane < half, ids[: listed // 2], ids[listed // 2 :] + half)
+    marked = hit.astype(f32)
     place = 0
     for r in range(strip):
         for h in range(cols // LANES):
             piece = mixed[r * planes : (r + 1) * planes, h * LANES : (h + 1) * LANES]
-            out[place] = jnp.where(lane < half, piece, listed).astype(bf16)
-            out[place + 1] = jnp.where(lane < half, pltpu.roll(piece, half, 1), listed).astype(bf16)
-            place += 2
+            piece = jnp.concatenate([piece, marked], axis=0).astype(bf16)
+            out[place] = piece
+            out[out.shape[0] // 2 + place] = piece
+            place += 1
 
 
 def weigh_body(block, first_row, defocus, groups, bin_planes, bin_tilts, received, images, out, square, chosen, centre, tilt, table, mixer, held, power):
@@ -133,7 +136,8 @@
             for g in range(0, group_total, rows):
                 mixed = dot(mixer[...], power[part, g : g + rows].reshape(rows * rows, cols), ((1,), (0,)))
                 square[:, part, g : g + rows, :] = mixed.astype(bf16).reshape(rows, rows, cols)
-        chosen[...] = received[...]
+        marked = received[...].astype(f32)[:, chosen.shape[1] :, :]
+        chosen[...] = jnp.concatenate([pltpu.roll(marked, LANES // 2, 2), marked], axis=1).astype(bf16)
         for q in range(centre.shape[0]):
             centre[q : q + 1, :] = jnp.full((1, LANES), bin_planes[q].astype(f32))
             tilt[q : q + 1, :] = jnp.full((1, LANES), bin_tilts[q])
@@ -151,23 +155,24 @@
     lax.fori_loop(0, block // rows, some, 0, unroll=True)
 
 
-def template_body(strip, height, row, centre, tilt, received, planes, out):
-    bands = planes.shape[0]
-    slab = planes.shape[1] // 2
+def template_body(strip, slab, height, row, group, centre, tilt, chosen, planes, out):
+    bands, both, _ = planes.shape
     bins = centre.shape[0]
+    peers, listed = out.shape[0], out.shape[1] // 2
     total = bands * slab
     where = lax.broadcasted_iota(jnp.int32, (bins, total), 1).astype(f32)
-    tables = []
+    picker = chosen[pl.ds(group[0] * peers, peers)].reshape(peers * listed, LANES)
+    values = planes[...].astype(f32)
+    empty = jnp.zeros((LANES - bins, LANES), bf16)
     for h in range(2):
         deep = centre[...] + tilt[...] * reach_of(row[0] + h * strip, slab, height)
         deep = jnp.concatenate([deep] * (total // LANES), axis=1)
         weight = jnp.maximum(0.0, 1.0 - jnp.abs(where - deep)).astype(bf16)
-        tables.append(dot(weight, planes[:, h * slab : (h + 1) * slab, :].reshape(total, LANES), ((1,), (0,))))
-    lane = lax.broadcasted_iota(jnp.int32, (bins, LANES), 1)
-    table = jnp.where(lane < LANES // 2, tables[0], pltpu.roll(tables[1], LANES // 2, 1))
-    table = jnp.concatenate([jnp.zeros((LANES - bins, LANES), bf16), table.astype(bf16)], axis=0)
-    chosen = received[...].reshape(-1, LANES)
-    out[...] = dot(chosen, table, ((1,), (0,))).astype(bf16).reshape(out.shape)
+        start = h * (both // 2)
+        rows = values[:, start : start + slab, :].reshape(total, LANES).astype(bf16)
+        table = jnp.concatenate([empty, dot(weight, rows, ((1,), (0,))).astype(bf16)], axis=0)
+        picked = dot(picker, table, ((1,), (0,))).astype(bf16)
+        out[:, h * listed : (h + 1) * listed, :] = picked.reshape(peers, listed, LANES)
 
 
 top = 32767.0
@@ -189,20 +194,14 @@
 def score_body(templates, weighted, square, out, extra):
     rows, images, cols = weighted.shape
     group_total = square.shape[0]
-    listed = templates.shape[1]
+    listed = templates.shape[1] // 2
     total = None
     power = None
-    lane = lax.broadcasted_iota(jnp.int32, (listed, LANES), 1)
-    pieces = [None] * rows
     strip = rows // 2
-    half = LANES // 2
-    for r in range(strip):
-        parts = [templates[4 * r + k].astype(f32) for k in range(4)]
-        turned = [pltpu.roll(part, half, 1) for part in parts]
-        pieces[r] = [jnp.where(lane < half, parts[k], turned[k + 1]) for k in (0, 2)]
-        pieces[strip + r] = [jnp.where(lane < half, turned[k], parts[k + 1]) for k in (0, 2)]
     for r in range(rows):
-        piece = jnp.concatenate(pieces[r], axis=1).astype(bf16)
+        start = r // strip * listed
+        piece = [templates[2 * (r % strip) + k, start : start + listed, :] for k in range(cols // LANES)]
+        piece = jnp.concatenate(piece, axis=1)
         part = dot(piece, weighted[r], ((1,), (1,)))
         total = part if total is None else total + part
         wide = piece.astype(f32)
@@ -271,11 +270,14 @@
     power = jnp.where(lane < 2 * group_total, power, 0.0)
     scale = 1.0 / jnp.sqrt(power + epsilon)
     scale = jnp.concatenate([scale, pltpu.roll(scale, LANES - group_total, 1)], axis=0)
-    member = lax.broadcasted_iota(jnp.int32, (LANES, images), 0) == groups[...]
-    member = member.astype(f32)
-    picked = lax.dot_general(
-        scale, member, (((1,), (0,)), ((), ())), precision=lax.Precision.HIGHEST, preferred_element_type=f32
-    )
+    parts = []
+    for _ in range(3):
+        parts.append(scale.astype(bf16))
+        scale = scale - parts[-1].astype(f32)
+    member = one_hot(lax.broadcasted_iota(jnp.int32, (group_total, images), 0) == groups[...])
+    member = jnp.concatenate([member, jnp.zeros((LANES - group_total, images), bf16)], axis=0)
+    picked = dot(jnp.concatenate(parts, axis=0), member, ((1,), (0,)))
+    picked = picked[:listed] + picked[listed : 2 * listed] + picked[2 * listed :]
     logits = sharpness[...] * scores * picked
     logits = jnp.exp(logits - jnp.max(logits, axis=0, keepdims=True))
     result = logits / jnp.sum(logits, axis=0, keepdims=True)
@@ -332,16 +334,19 @@
     bins = bin_planes.shape[0]
     listed = bin_lists.shape[1]
     group_total = defocus.shape[0]
+    lane_halves = cols // LANES
     first_row = row_of(rows).reshape(1)
 
+    piece_rows = planes + listed // 2
+    half_group = blocks // 2
     sent = call(
         part_body,
-        pltpu.VMEM((blocks, planes, LANES), bf16),
+        pltpu.VMEM((blocks, piece_rows, LANES), bf16),
         [VMEM, VMEM],
         VMEM,
     )(*in_hbm(bin_lists, volume))
     received = lax.all_to_all(sent, "img", 0, 0, tiled=True)
-    stack = lax.all_to_all(received.reshape(bands, 2 * planes, LANES), "vol", 0, 0, tiled=True)
+    stack = lax.all_to_all(received.reshape(bands, 2 * piece_rows, LANES), "vol", 0, 0, tiled=True)
 
     block = 256
     weighted, square, chosen, centre, tilt = call(
@@ -349,19 +354,19 @@
         (
             pltpu.HBM((rows, image_count, cols), bf16),
             jax.ShapeDtypeStruct((rows, 2, group_total, cols), bf16),
-            jax.ShapeDtypeStruct((blocks, planes, LANES), bf16),
+            jax.ShapeDtypeStruct((blocks, listed, LANES), bf16),
             jax.ShapeDtypeStruct((bins, LANES), f32),
             jax.ShapeDtypeStruct((bins, LANES), f32),
         ),
         [SMEM] * 5
         + [
-            pl.BlockSpec((blocks, planes, LANES), lambda i: (0, 0, 0)),
+            pl.BlockSpec((blocks, piece_rows, LANES), lambda i: (0, 0, 0)),
             pl.BlockSpec((block, rows, cols), lambda i: (i, 0, 0)),
         ],
         (
             pl.BlockSpec((rows, block, cols), lambda i: (0, i, 0)),
             pl.BlockSpec((rows, 2, group_total, cols), lambda i: (0, 0, 0, 0)),
-            pl.BlockSpec((blocks, planes, LANES), lambda i: (0, 0, 0)),
+            pl.BlockSpec((blocks, listed, LANES), lambda i: (0, 0, 0)),
             pl.BlockSpec((bins, LANES), lambda i: (0, 0)),
             pl.BlockSpec((bins, LANES), lambda i: (0, 0)),
         ),
@@ -376,15 +381,19 @@
         nbytes=4 * image_count * rows * cols,
     )(first_row, *in_hbm(defocus, groups, bin_planes, bin_tilts, received, images))
 
+    img_index = lax.axis_index("img")
+    own_row = first_row + img_index % half_group // lane_halves
+    own_group = (img_index // half_group).reshape(1)
     pieces = call(
-        functools.partial(template_body, strip, height),
-        jax.ShapeDtypeStruct((blocks, listed, LANES), bf16),
-        [SMEM, VMEM, VMEM, VMEM, VMEM],
+        functools.partial(template_body, strip, planes, height),
+        jax.ShapeDtypeStruct((half_group, 2 * listed, LANES), bf16),
+        [SMEM, SMEM, VMEM, VMEM, VMEM, VMEM],
         VMEM,
         flops=2**33,
         nbytes=2**25,
-    )(first_row + lax.axis_index("img") // 4, centre, tilt, chosen, stack)
-    templates = lax.all_to_all(pieces, "img", 0, 0, tiled=True)
+    )(own_row, own_group, centre, tilt, chosen, stack)
+    halves = [list(range(half_group)), list(range(half_group, blocks))]
+    templates = lax.all_to_all(pieces, "img", 0, 0, tiled=True, axis_index_groups=halves)
 
     payload_rows = listed * (image_count // LANES + 1)
     partial = call(

time: 105 us -> 105 us (level)
    all_to_all x1, blocking collectives: 15.9 us -> 13.3 us  [per_device(): lax.all_to_all(pieces, 'img', 0, 0, tiled=True, axis_index_groups=halves)]
    all_to_all x1, blocking collectives: 15.8 us -> 17.4 us  [per_device(): arrived = lax.all_to_all(spread, 'img', 0, 0, tiled=True)]
    all_to_all x1, blocking collectives: 25.7 us -> 26.9 us  [per_device(): received = lax.all_to_all(sent, 'img', 0, 0, tiled=True)]
where the time goes in v5:
time: 105 us
  blocking collectives  83.3 us (79%)
  Pallas kernels  11.4 us (11%)
  starting transfers between devices  7.2 us (7%)
  waiting for transfers between devices  2.06 us (2%)
    all_to_all x1, blocking collectives, per_device(): received = lax.all_to_all(sent, 'img', 0, 0, tiled=True)  26.9 us
    all_to_all x1, blocking collectives, per_device(): arrived = lax.all_to_all(spread, 'img', 0, 0, tiled=True)  17.4 us
    all_to_all x1, blocking collectives, per_device(): partial = lax.all_to_all(partial, 'vol', 0, 0, tiled=True)  14.1 us
    all_to_all x1, blocking collectives, per_device(): lax.all_to_all(pieces, 'img', 0, 0, tiled=True, axis_index_groups=halves)  13.3 us
    all_to_all x1, blocking collectives, per_device(): slabs = lax.all_to_all(projected, 'vol', 0, 0, tiled=True)  11.5 us
    all_to_all x1, starting transfers between devices, per_device(): lax.all_to_all(received.reshape(bands, 2 * piece_rows, LANES), 'vol', 0,...  7.2 us
    pallas_call x1, Pallas kernels, per_device(): call(functools.partial(weigh_body, block), (pltpu.HBM((rows, image_count,...  5.47 us
  transfers between devices with their start and end apart: 1, of which 1 were waited for; matrix products, arithmetic and copies ran while one was open for 0% of the time, Pallas kernels for 5%

profile of v5, /device:TPU:1, one launch (start us, length us, event | category | flops | bytes accessed | tf_op | source)
XLA Modules:
  0.0 104.7 jit_solution(14958310483395653239)
XLA Ops:
  0.6 1.0 shard_map.95
  1.6 26.9 %all_to_all.30.received = bf16[32,24,128]{2,1,0:T(8,128)(2,1)} all-to-all(bf16[32,24,128]{2,1,0:T(8,128)(2,1)S(1)} %shard_map.95), channel_id=1, replica_groups=mesh['vol'=16,'img'=32] {'img'}, dimensions={0} | all-to-all | bytes 393216 | tf_op jit(solution)/shard_map/all_to_all | solution.py:348
  28.5 7.2 %all-to-all-start.1 = ((bf16[16,48,128]{2,1,0:T(8,128)(2,1)}), bf16[16,48,128]{2,1,0:T(8,128)(2,1)S(1)}, u32[]{:S(2)}, u32[]{:S(2)}) async-start(bf16[16,48,128]{2,1,0:T(8,128)(2,1)} %bitcast.3), calls=%async_computation.1 | async-start | bytes 393216 | tf_op jit(solution)/shard_map/all_to_all | solution.py:349
  35.8 5.5 %shard_map.96 = (bf16[16,512,256]{2,1,0:T(8,128)(2,1)}, bf16[16,2,32,256]{3,2,1,0:T(8,128)(2,1)S(1)}, bf16[32,16,128]{2,1,0:T(8,128)(2,1)S(1)}, f32[64,128]{1,0:T(8,128)S(1)}, f32[64,128]{1,0:T(8,128)S(1)}) custom-call(s32[1]{0:T(128)} %bitcast.first_row, f32[32]{0:T(128)} %defocus.1, s32[512]{0:T(512)} %groups.1, s32[64]{0:T(128)} %bin_planes.1, ...), custom_call_target="tpu_custom_call" | custom-call | flops 83886080 | bytes 8388608 | tf_op jit(solution)/shard_map/pallas_call | solution.py:352
  41.3 2.1 %all-to-all-done.1.planes = bf16[16,48,128]{2,1,0:T(8,128)(2,1)S(1)} async-done(((bf16[16,48,128]{2,1,0:T(8,128)(2,1)}), bf16[16,48,128]{2,1,0:T(8,128)(2,1)S(1)}, u32[]{:S(2)}, u32[]{:S(2)}) %all-to-all-start.1) | async-done | bytes 196640 | tf_op jit(solution)/shard_map/all_to_all | solution.py:349
  43.3 0.0 copy-start
  43.3 0.3 shard_map.97
  43.7 0.0 copy-start.1
  43.7 0.0 copy-start.2
  43.7 13.3 %all_to_all.31.templates = bf16[16,32,128]{2,1,0:T(8,128)(2,1)S(1)} all-to-all(bf16[16,32,128]{2,1,0:T(8,128)(2,1)S(1)} %shard_map.97), channel_id=1, replica_groups={{0,1,2,3,4,5,6,7,8,9,10,11,12,13,14,15},{16,17,18,19,20,21,22,23,24,25,..., dimensions={0} | all-to-all | bytes 262144 | tf_op jit(solution)/shard_map/all_to_all | solution.py:396
  57.0 0.0 copy-done
  57.0 1.6 %shard_map.98 = s16[16,80,128]{2,1,0:T(8,128)(2,1)S(1)} custom-call(bf16[16,32,128]{2,1,0:T(8,128)(2,1)S(1)} %all_to_all.31.templates, bf16[16,512,256]{2,1,0:T(8,128)(2,1)S(1)} %copy-done, bf16[16,2,32,256]{3,2,1,0:T(8,128)(2,1)S(1)} %get-tuple-element.13.square), custom_call_target="tpu_custom_call" | custom-call | tf_op jit(solution)/shard_map/pallas_call | solution.py:399
  58.6 14.1 %all_to_all.32.partial = s16[16,80,128]{2,1,0:T(8,128)(2,1)S(1)} all-to-all(s16[16,80,128]{2,1,0:T(8,128)(2,1)S(1)} %shard_map.98), channel_id=1, replica_groups=mesh['vol'=16,'img'=32] {'vol'}, dimensions={0} | all-to-all | bytes 655360 | tf_op jit(solution)/shard_map/all_to_all | solution.py:406
  72.7 0.0 copy-done.1
  72.7 0.0 copy-done.2
  72.7 1.4 %shard_map.99 = (f32[16,512]{1,0:T(8,128)}, bf16[32,16,128]{2,1,0:T(8,128)(2,1)S(1)}) custom-call(s16[16,80,128]{2,1,0:T(8,128)(2,1)S(1)} %all_to_all.32.partial, s32[1,512]{1,0:T(1,128)S(1)} %bitcast.8, f32[1,512]{1,0:T(1,128)S(1)} %bitcast.9, bf16[16,512,256]{2,1,0:T(8,128)(2,1)S(1)} %copy-done), custom_call_target="tpu_custom_call" | custom-call | tf_op jit(solution)/shard_map/pallas_call | solution.py:408
  74.1 17.4 %all_to_all.33.arrived = bf16[32,16,128]{2,1,0:T(8,128)(2,1)S(1)} all-to-all(bf16[32,16,128]{2,1,0:T(8,128)(2,1)S(1)} %get-tuple-element.15), channel_id=1, replica_groups=mesh['vol'=16,'img'=32] {'img'}, dimensions={0} | all-to-all | bytes 262144 | tf_op jit(solution)/shard_map/all_to_all | solution.py:417
  91.5 0.7 shard_map.100
  92.3 11.5 %all_to_all.34.arrived = bf16[16,16,128]{2,1,0:T(8,128)(2,1)S(1)} all-to-all(bf16[16,16,128]{2,1,0:T(8,128)(2,1)S(1)} %shard_map.100), channel_id=1, replica_groups=mesh['vol'=16,'img'=32] {'vol'}, dimensions={0} | all-to-all | bytes 131072 | tf_op jit(solution)/shard_map/all_to_all | solution.py:425
  103.8 0.9 shard_map.101
Async XLA Ops:
  28.5 14.8 %all-to-all-start.1 = ((bf16[16,48,128]{2,1,0:T(8,128)(2,1)}), bf16[16,48,128]{2,1,0:T(8,128)(2,1)S(1)}, u32[]{:S(2)}, u32[]{:S(2)}) async-start(bf16[16,48,128]{2,1,0:T(8,128)(2,1)} %bitcast.3), calls=%async_computation.1 | async-start | bytes 393216 | tf_op jit(solution)/shard_map/all_to_all | solution.py:349
  43.3 13.7 %copy-start = (bf16[16,512,256]{2,1,0:T(8,128)(2,1)S(1)}, bf16[16,512,256]{2,1,0:T(8,128)(2,1)}, u32[]{:S(2)}) copy-start(bf16[16,512,256]{2,1,0:T(8,128)(2,1)} %get-tuple-element.12.weighted) | copy-start | bytes 12582916
  43.7 29.0 %copy-start.1 = (s32[512]{0:T(512)S(1)}, s32[512]{0:T(512)}, u32[]{:S(2)}) copy-start(s32[512]{0:T(512)} %groups.1) | copy-start | bytes 6148
  43.7 29.0 %copy-start.2 = (f32[512]{0:T(512)S(1)}, f32[512]{0:T(512)}, u32[]{:S(2)}) copy-start(f32[512]{0:T(512)} %param.15) | copy-start | bytes 6148

commit v6 on v5

--- a/solution.py
+++ b/solution.py
@@ -346,7 +346,7 @@
         VMEM,
     )(*in_hbm(bin_lists, volume))
     received = lax.all_to_all(sent, "img", 0, 0, tiled=True)
-    stack = lax.all_to_all(received.reshape(bands, 2 * piece_rows, LANES), "vol", 0, 0, tiled=True)
+    stack = lax.all_to_all(received[:, :planes].reshape(bands, 2 * planes, LANES), "vol", 0, 0, tiled=True)
 
     block = 256
     weighted, square, chosen, centre, tilt = call(

time: 105 us -> 105 us (level)
  no operation moved by 1% of the time
where the time goes in v6:
time: 105 us; the launch traced here: 104 us
  blocking collectives  82.3 us (78%)
  Pallas kernels  11.4 us (11%)
  starting transfers between devices  7.2 us (7%)
  waiting for transfers between devices  2.03 us (2%)
    all_to_all x1, blocking collectives, per_device(): received = lax.all_to_all(sent, 'img', 0, 0, tiled=True)  26.8 us
    all_to_all x1, blocking collectives, per_device(): arrived = lax.all_to_all(spread, 'img', 0, 0, tiled=True)  17.9 us
    all_to_all x1, blocking collectives, per_device(): partial = lax.all_to_all(partial, 'vol', 0, 0, tiled=True)  13.2 us
    all_to_all x1, blocking collectives, per_device(): lax.all_to_all(pieces, 'img', 0, 0, tiled=True, axis_index_groups=halves)  12.8 us
    all_to_all x1, blocking collectives, per_device(): slabs = lax.all_to_all(projected, 'vol', 0, 0, tiled=True)  11.6 us
    all_to_all x1, starting transfers between devices, per_device(): lax.all_to_all(received[:, :planes].reshape(bands, 2 * planes, LANES), 'v...  7.2 us
    pallas_call x1, Pallas kernels, per_device(): call(functools.partial(weigh_body, block), (pltpu.HBM((rows, image_count,...  5.44 us
  transfers between devices with their start and end apart: 1, of which 1 were waited for; matrix products, arithmetic and copies ran while one was open for 0% of the time, Pallas kernels for 5%

profile of v6, /device:TPU:1, one launch (start us, length us, event | category | flops | bytes accessed | tf_op | source)
XLA Modules:
  0.0 104.3 jit_solution(11329411137785178445)
XLA Ops:
  0.6 1.0 shard_map.95
  1.6 26.8 %all_to_all.30.received = bf16[32,24,128]{2,1,0:T(8,128)(2,1)S(1)} all-to-all(bf16[32,24,128]{2,1,0:T(8,128)(2,1)S(1)} %shard_map.95), channel_id=1, replica_groups=mesh['vol'=16,'img'=32] {'img'}, dimensions={0} | all-to-all | bytes 393216 | tf_op jit(solution)/shard_map/all_to_all | solution.py:348
  28.4 0.0 copy-start.3
  28.4 0.7 slice.4
  29.1 7.2 %all-to-all-start.1 = ((bf16[16,32,128]{2,1,0:T(8,128)(2,1)}), bf16[16,32,128]{2,1,0:T(8,128)(2,1)S(1)}, u32[]{:S(2)}, u32[]{:S(2)}) async-start(bf16[16,32,128]{2,1,0:T(8,128)(2,1)} %bitcast.3), calls=%async_computation.1 | async-start | bytes 262144 | tf_op jit(solution)/shard_map/all_to_all | solution.py:349
  36.4 0.0 copy-done.3
  36.4 5.4 %shard_map.96 = (bf16[16,512,256]{2,1,0:T(8,128)(2,1)}, bf16[16,2,32,256]{3,2,1,0:T(8,128)(2,1)S(1)}, bf16[32,16,128]{2,1,0:T(8,128)(2,1)S(1)}, f32[64,128]{1,0:T(8,128)S(1)}, f32[64,128]{1,0:T(8,128)S(1)}) custom-call(s32[1]{0:T(128)} %bitcast.first_row, f32[32]{0:T(128)} %defocus.1, s32[512]{0:T(512)} %groups.1, s32[64]{0:T(128)} %bin_planes.1, ...), custom_call_target="tpu_custom_call" | custom-call | flops 83886080 | bytes 8388608 | tf_op jit(solution)/shard_map/pallas_call | solution.py:352
  41.8 2.0 %all-to-all-done.1.planes = bf16[16,32,128]{2,1,0:T(8,128)(2,1)S(1)} async-done(((bf16[16,32,128]{2,1,0:T(8,128)(2,1)}), bf16[16,32,128]{2,1,0:T(8,128)(2,1)S(1)}, u32[]{:S(2)}, u32[]{:S(2)}) %all-to-all-start.1) | async-done | bytes 131104 | tf_op jit(solution)/shard_map/all_to_all | solution.py:349
  43.9 0.0 copy-start
  43.9 0.3 shard_map.97
  44.2 0.0 copy-start.1
  44.2 0.0 copy-start.2
  44.2 12.8 %all_to_all.31.templates = bf16[16,32,128]{2,1,0:T(8,128)(2,1)S(1)} all-to-all(bf16[16,32,128]{2,1,0:T(8,128)(2,1)S(1)} %shard_map.97), channel_id=1, replica_groups={{0,1,2,3,4,5,6,7,8,9,10,11,12,13,14,15},{16,17,18,19,20,21,22,23,24,25,..., dimensions={0} | all-to-all | bytes 262144 | tf_op jit(solution)/shard_map/all_to_all | solution.py:396
  57.1 0.0 copy-done
  57.1 1.6 %shard_map.98 = s16[16,80,128]{2,1,0:T(8,128)(2,1)S(1)} custom-call(bf16[16,32,128]{2,1,0:T(8,128)(2,1)S(1)} %all_to_all.31.templates, bf16[16,512,256]{2,1,0:T(8,128)(2,1)S(1)} %copy-done, bf16[16,2,32,256]{3,2,1,0:T(8,128)(2,1)S(1)} %get-tuple-element.13.square), custom_call_target="tpu_custom_call" | custom-call | tf_op jit(solution)/shard_map/pallas_call | solution.py:399
  58.6 13.2 %all_to_all.32.partial = s16[16,80,128]{2,1,0:T(8,128)(2,1)S(1)} all-to-all(s16[16,80,128]{2,1,0:T(8,128)(2,1)S(1)} %shard_map.98), channel_id=1, replica_groups=mesh['vol'=16,'img'=32] {'vol'}, dimensions={0} | all-to-all | bytes 655360 | tf_op jit(solution)/shard_map/all_to_all | solution.py:406
  71.9 0.0 copy-done.1
  71.9 0.0 copy-done.2
  71.9 1.4 %shard_map.99 = (f32[16,512]{1,0:T(8,128)}, bf16[32,16,128]{2,1,0:T(8,128)(2,1)S(1)}) custom-call(s16[16,80,128]{2,1,0:T(8,128)(2,1)S(1)} %all_to_all.32.partial, s32[1,512]{1,0:T(1,128)S(1)} %bitcast.8, f32[1,512]{1,0:T(1,128)S(1)} %bitcast.9, bf16[16,512,256]{2,1,0:T(8,128)(2,1)S(1)} %copy-done), custom_call_target="tpu_custom_call" | custom-call | tf_op jit(solution)/shard_map/pallas_call | solution.py:408
  73.3 17.9 %all_to_all.33.arrived = bf16[32,16,128]{2,1,0:T(8,128)(2,1)S(1)} all-to-all(bf16[32,16,128]{2,1,0:T(8,128)(2,1)S(1)} %get-tuple-element.15), channel_id=1, replica_groups=mesh['vol'=16,'img'=32] {'img'}, dimensions={0} | all-to-all | bytes 262144 | tf_op jit(solution)/shard_map/all_to_all | solution.py:417
  91.2 0.7 shard_map.100
  91.9 11.6 %all_to_all.34.arrived = bf16[16,16,128]{2,1,0:T(8,128)(2,1)S(1)} all-to-all(bf16[16,16,128]{2,1,0:T(8,128)(2,1)S(1)} %shard_map.100), channel_id=1, replica_groups=mesh['vol'=16,'img'=32] {'vol'}, dimensions={0} | all-to-all | bytes 131072 | tf_op jit(solution)/shard_map/all_to_all | solution.py:425
  103.5 0.9 shard_map.101
Async XLA Ops:
  28.4 8.0 %copy-start.3 = (bf16[32,24,128]{2,1,0:T(8,128)(2,1)}, bf16[32,24,128]{2,1,0:T(8,128)(2,1)S(1)}, u32[]{:S(2)}) copy-start(bf16[32,24,128]{2,1,0:T(8,128)(2,1)S(1)} %all_to_all.30.received) | copy-start | bytes 589828
  29.1 14.7 %all-to-all-start.1 = ((bf16[16,32,128]{2,1,0:T(8,128)(2,1)}), bf16[16,32,128]{2,1,0:T(8,128)(2,1)S(1)}, u32[]{:S(2)}, u32[]{:S(2)}) async-start(bf16[16,32,128]{2,1,0:T(8,128)(2,1)} %bitcast.3), calls=%async_computation.1 | async-start | bytes 262144 | tf_op jit(solution)/shard_map/all_to_all | solution.py:349
  43.9 13.2 %copy-start = (bf16[16,512,256]{2,1,0:T(8,128)(2,1)S(1)}, bf16[16,512,256]{2,1,0:T(8,128)(2,1)}, u32[]{:S(2)}) copy-start(bf16[16,512,256]{2,1,0:T(8,128)(2,1)} %get-tuple-element.12.weighted) | copy-start | bytes 12582916
  44.2 27.7 %copy-start.1 = (s32[512]{0:T(512)S(1)}, s32[512]{0:T(512)}, u32[]{:S(2)}) copy-start(s32[512]{0:T(512)} %groups.1) | copy-start | bytes 6148
  44.2 27.7 %copy-start.2 = (f32[512]{0:T(512)S(1)}, f32[512]{0:T(512)}, u32[]{:S(2)}) copy-start(f32[512]{0:T(512)} %param.15) | copy-start | bytes 6148

commit v7 on v5

--- a/solution.py
+++ b/solution.py
@@ -258,8 +258,9 @@
         extra = value[chunks * listed :]
         place = half + chunks
         power_code = jnp.sum(jnp.where(square_mask, extra[place : place + 1], 0.0), axis=1, keepdims=True)
-        row_level = level_of(0.5 * power_code) * (1.0 / top)
-        power_level = level_of(power_code) * (1.0 / top)
+        row_level = level_of(0.5 * power_code)
+        power_level = row_level * row_level * (1.0 / top)
+        row_level = row_level * (1.0 / top)
         image_level = [level_of(extra[half + c : half + c + 1]) for c in range(chunks)]
         part = [value[c * listed : (c + 1) * listed] * row_level * image_level[c] for c in range(chunks)]
         scores = part if scores is None else [a + b for a, b in zip(scores, part)]

time: 105 us -> 105 us (level)
  no operation moved by 1% of the time
where the time goes in v7:
time: 105 us
  blocking collectives  83.3 us (79%)
  Pallas kernels  11.4 us (11%)
  starting transfers between devices  7.2 us (7%)
  waiting for transfers between devices  2.06 us (2%)
    all_to_all x1, blocking collectives, per_device(): received = lax.all_to_all(sent, 'img', 0, 0, tiled=True)  26.9 us
    all_to_all x1, blocking collectives, per_device(): arrived = lax.all_to_all(spread, 'img', 0, 0, tiled=True)  17.4 us
    all_to_all x1, blocking collectives, per_device(): partial = lax.all_to_all(partial, 'vol', 0, 0, tiled=True)  14.1 us
    all_to_all x1, blocking collectives, per_device(): lax.all_to_all(pieces, 'img', 0, 0, tiled=True, axis_index_groups=halves)  13.3 us
    all_to_all x1, blocking collectives, per_device(): slabs = lax.all_to_all(projected, 'vol', 0, 0, tiled=True)  11.5 us
    all_to_all x1, starting transfers between devices, per_device(): lax.all_to_all(received.reshape(bands, 2 * piece_rows, LANES), 'vol', 0,...  7.2 us
    pallas_call x1, Pallas kernels, per_device(): call(functools.partial(weigh_body, block), (pltpu.HBM((rows, image_count,...  5.47 us
  transfers between devices with their start and end apart: 1, of which 1 were waited for; matrix products, arithmetic and copies ran while one was open for 0% of the time, Pallas kernels for 5%

profile of v7, /device:TPU:1, one launch (start us, length us, event | category | flops | bytes accessed | tf_op | source)
XLA Modules:
  0.0 104.6 jit_solution(11244047340174083213)
XLA Ops:
  0.6 1.0 shard_map.95
  1.6 26.9 %all_to_all.30.received = bf16[32,24,128]{2,1,0:T(8,128)(2,1)} all-to-all(bf16[32,24,128]{2,1,0:T(8,128)(2,1)S(1)} %shard_map.95), channel_id=1, replica_groups=mesh['vol'=16,'img'=32] {'img'}, dimensions={0} | all-to-all | bytes 393216 | tf_op jit(solution)/shard_map/all_to_all | solution.py:349
  28.5 7.2 %all-to-all-start.1 = ((bf16[16,48,128]{2,1,0:T(8,128)(2,1)}), bf16[16,48,128]{2,1,0:T(8,128)(2,1)S(1)}, u32[]{:S(2)}, u32[]{:S(2)}) async-start(bf16[16,48,128]{2,1,0:T(8,128)(2,1)} %bitcast.3), calls=%async_computation.1 | async-start | bytes 393216 | tf_op jit(solution)/shard_map/all_to_all | solution.py:350
  35.8 5.5 %shard_map.96 = (bf16[16,512,256]{2,1,0:T(8,128)(2,1)}, bf16[16,2,32,256]{3,2,1,0:T(8,128)(2,1)S(1)}, bf16[32,16,128]{2,1,0:T(8,128)(2,1)S(1)}, f32[64,128]{1,0:T(8,128)S(1)}, f32[64,128]{1,0:T(8,128)S(1)}) custom-call(s32[1]{0:T(128)} %bitcast.first_row, f32[32]{0:T(128)} %defocus.1, s32[512]{0:T(512)} %groups.1, s32[64]{0:T(128)} %bin_planes.1, ...), custom_call_target="tpu_custom_call" | custom-call | flops 83886080 | bytes 8388608 | tf_op jit(solution)/shard_map/pallas_call | solution.py:353
  41.3 2.1 %all-to-all-done.1.planes = bf16[16,48,128]{2,1,0:T(8,128)(2,1)S(1)} async-done(((bf16[16,48,128]{2,1,0:T(8,128)(2,1)}), bf16[16,48,128]{2,1,0:T(8,128)(2,1)S(1)}, u32[]{:S(2)}, u32[]{:S(2)}) %all-to-all-start.1) | async-done | bytes 196640 | tf_op jit(solution)/shard_map/all_to_all | solution.py:350
  43.3 0.0 copy-start
  43.3 0.3 shard_map.97
  43.7 0.0 copy-start.1
  43.7 0.0 copy-start.2
  43.7 13.3 %all_to_all.31.templates = bf16[16,32,128]{2,1,0:T(8,128)(2,1)S(1)} all-to-all(bf16[16,32,128]{2,1,0:T(8,128)(2,1)S(1)} %shard_map.97), channel_id=1, replica_groups={{0,1,2,3,4,5,6,7,8,9,10,11,12,13,14,15},{16,17,18,19,20,21,22,23,24,25,..., dimensions={0} | all-to-all | bytes 262144 | tf_op jit(solution)/shard_map/all_to_all | solution.py:397
  57.0 0.0 copy-done
  57.0 1.6 %shard_map.98 = s16[16,80,128]{2,1,0:T(8,128)(2,1)S(1)} custom-call(bf16[16,32,128]{2,1,0:T(8,128)(2,1)S(1)} %all_to_all.31.templates, bf16[16,512,256]{2,1,0:T(8,128)(2,1)S(1)} %copy-done, bf16[16,2,32,256]{3,2,1,0:T(8,128)(2,1)S(1)} %get-tuple-element.13.square), custom_call_target="tpu_custom_call" | custom-call | tf_op jit(solution)/shard_map/pallas_call | solution.py:400
  58.6 14.1 %all_to_all.32.partial = s16[16,80,128]{2,1,0:T(8,128)(2,1)S(1)} all-to-all(s16[16,80,128]{2,1,0:T(8,128)(2,1)S(1)} %shard_map.98), channel_id=1, replica_groups=mesh['vol'=16,'img'=32] {'vol'}, dimensions={0} | all-to-all | bytes 655360 | tf_op jit(solution)/shard_map/all_to_all | solution.py:407
  72.7 0.0 copy-done.1
  72.7 0.0 copy-done.2
  72.7 1.4 %shard_map.99 = (f32[16,512]{1,0:T(8,128)}, bf16[32,16,128]{2,1,0:T(8,128)(2,1)S(1)}) custom-call(s16[16,80,128]{2,1,0:T(8,128)(2,1)S(1)} %all_to_all.32.partial, s32[1,512]{1,0:T(1,128)S(1)} %bitcast.8, f32[1,512]{1,0:T(1,128)S(1)} %bitcast.9, bf16[16,512,256]{2,1,0:T(8,128)(2,1)S(1)} %copy-done), custom_call_target="tpu_custom_call" | custom-call | tf_op jit(solution)/shard_map/pallas_call | solution.py:409
  74.1 17.4 %all_to_all.33.arrived = bf16[32,16,128]{2,1,0:T(8,128)(2,1)S(1)} all-to-all(bf16[32,16,128]{2,1,0:T(8,128)(2,1)S(1)} %get-tuple-element.15), channel_id=1, replica_groups=mesh['vol'=16,'img'=32] {'img'}, dimensions={0} | all-to-all | bytes 262144 | tf_op jit(solution)/shard_map/all_to_all | solution.py:418
  91.5 0.7 shard_map.100
  92.2 11.5 %all_to_all.34.arrived = bf16[16,16,128]{2,1,0:T(8,128)(2,1)S(1)} all-to-all(bf16[16,16,128]{2,1,0:T(8,128)(2,1)S(1)} %shard_map.100), channel_id=1, replica_groups=mesh['vol'=16,'img'=32] {'vol'}, dimensions={0} | all-to-all | bytes 131072 | tf_op jit(solution)/shard_map/all_to_all | solution.py:426
  103.8 0.9 shard_map.101
Async XLA Ops:
  28.5 14.8 %all-to-all-start.1 = ((bf16[16,48,128]{2,1,0:T(8,128)(2,1)}), bf16[16,48,128]{2,1,0:T(8,128)(2,1)S(1)}, u32[]{:S(2)}, u32[]{:S(2)}) async-start(bf16[16,48,128]{2,1,0:T(8,128)(2,1)} %bitcast.3), calls=%async_computation.1 | async-start | bytes 393216 | tf_op jit(solution)/shard_map/all_to_all | solution.py:350
  43.3 13.7 %copy-start = (bf16[16,512,256]{2,1,0:T(8,128)(2,1)S(1)}, bf16[16,512,256]{2,1,0:T(8,128)(2,1)}, u32[]{:S(2)}) copy-start(bf16[16,512,256]{2,1,0:T(8,128)(2,1)} %get-tuple-element.12.weighted) | copy-start | bytes 12582916
  43.7 29.0 %copy-start.1 = (s32[512]{0:T(512)S(1)}, s32[512]{0:T(512)}, u32[]{:S(2)}) copy-start(s32[512]{0:T(512)} %groups.1) | copy-start | bytes 6148
  43.7 29.0 %copy-start.2 = (f32[512]{0:T(512)S(1)}, f32[512]{0:T(512)}, u32[]{:S(2)}) copy-start(f32[512]{0:T(512)} %param.15) | copy-start | bytes 6148
